TPU v7x, 128 devices: a whole 4x4x4 slice. The times are simulated.
128 devices in a mesh: seq: 16 (over x, z_lo, core), head: 8 (over y, z_hi).
Axes of the slice: x: 4, y: 4, z: 4 (z_hi: 2, z_lo: 2; z = z_hi * 2 + z_lo), core: 2. Of those that a mesh axis runs over, the one named last changes fastest.
Arguments:
- q_nope: bfloat16 [4096, 16384], P('seq', 'head'), may hold values from -6 to 6
- q_rope: bfloat16 [4096, 8192], P('seq', 'head'), may hold values from -120 to 120
- latent: bfloat16 [4096, 512], P(('seq', 'head')), may hold values from -6 to 6
- k_rope: bfloat16 [4096, 64], P(('seq', 'head')), may hold values from -4 to 4
- positions: int32 [4096], P('seq'), may hold values from 0 to 4095, as said below
- w_uk: bfloat16 [512, 16384], P(None, 'head'), may hold values from -0.25 to 0.25
- w_uv: bfloat16 [512, 16384], P(None, 'head'), may hold values from -0.25 to 0.25
Outputs:
- attended: bfloat16 [4096, 16384], P('seq', 'head')
Inputs may be any that keep to these rules, and one draw needn't show every extreme that they name: positions is a permutation of 0 to 4095 made of 32 aligned runs of 128 rows, each run holding 128 consecutive rising positions; which block sits where is drawn.
All inputs are finite; a program needn't handle non-finite values.
Results may differ from a plain program's by a relative error of at most 0.0073.
Values may be sent and summed in bfloat16 or wider, within the bound.
A program may use at most 64 MiB of HBM per device.

v0:
```python
import jax
import jax.numpy as jnp
from jax import lax
from jax.sharding import PartitionSpec as P

NOPE = 128
ROPE = 64
VDIM = 128


def from_behind(block, axis, distance):
    devices = range(lax.axis_size(axis))
    route = [((i - distance) % len(devices), i) for i in devices]
    return lax.ppermute(block, axis, route)


def per_device(q_nope, q_rope, latent, k_rope, positions, w_uk, w_uv):
    scale = (NOPE + ROPE) ** (-0.5)
    local_rows = q_nope.shape[0]
    heads_here = w_uk.shape[1] // NOPE
    query_plain = q_nope.reshape(local_rows, heads_here, NOPE)
    query_rot = q_rope.reshape(local_rows, heads_here, ROPE)
    latent_all, rope_all = (
        lax.all_gather(latent, "head", axis=0, tiled=True),
        lax.all_gather(k_rope, "head", axis=0, tiled=True),
    )
    own_block = (latent_all, rope_all, positions)

    def update(state, block):
        lat_rows, rot_rows, key_pos = block
        count = lat_rows.shape[0]

        def compute(carried):
            top, total, accum = carried
            keys = jnp.dot(lat_rows, w_uk, preferred_element_type=jnp.float32).astype(jnp.bfloat16)
            values = jnp.dot(lat_rows, w_uv, preferred_element_type=jnp.float32).astype(
                jnp.bfloat16
            )
            keys = keys.reshape(count, heads_here, NOPE)
            values = values.reshape(count, heads_here, VDIM)
            scores = jnp.einsum(
                "qhd,khd->hqk", query_plain, keys, preferred_element_type=jnp.float32
            )
            scores = (
                scores
                + jnp.einsum("qhd,kd->hqk", query_rot, rot_rows, preferred_element_type=jnp.float32)
            ) * scale
            allowed = (key_pos[None, :] <= positions[:, None])[None, :, :]
            scores = jnp.where(allowed, scores, -1e30)
            new_top = jnp.maximum(top, jnp.max(scores, axis=2))
            weights = jnp.where(allowed, jnp.exp(scores - new_top[:, :, None]), 0.0)
            factor = jnp.exp(top - new_top)
            total = total * factor + jnp.sum(weights, axis=2)
            accum = accum * factor[:, :, None] + jnp.einsum(
                "hqk,khd->hqd",
                weights.astype(jnp.bfloat16),
                values,
                preferred_element_type=jnp.float32,
            )
            return (new_top, total, accum)

        needed = jnp.min(key_pos) <= jnp.max(positions)
        return lax.cond(needed, compute, lambda carried: carried, state)

    start_state = (
        jnp.full((heads_here, local_rows), -1e30, jnp.float32),
        jnp.zeros((heads_here, local_rows), jnp.float32),
        jnp.zeros((heads_here, local_rows, VDIM), jnp.float32),
    )
    cycle_len = lax.axis_size("seq")
    state = update(start_state, own_block)

    def cycle_turn(step, carry):
        state_now, block = carry
        block = from_behind((block[0], block[1], block[2]), "seq", 1)
        return (update(state_now, block), block)

    state, unused_block = lax.fori_loop(0, cycle_len - 1, cycle_turn, (state, own_block))
    top, total, accum = state
    output = accum / total[:, :, None]
    return (
        jnp.transpose(output, (1, 0, 2)).reshape(local_rows, heads_here * VDIM).astype(jnp.bfloat16)
    )


def solution(mesh):
    in_specs = (
        P("seq", "head"),
        P("seq", "head"),
        P(("seq", "head"), None),
        P(("seq", "head"), None),
        P("seq"),
        P(None, "head"),
        P(None, "head"),
    )
    out_specs = P("seq", "head")
    return jax.shard_map(
        per_device, mesh=mesh, in_specs=in_specs, out_specs=out_specs, check_vma=False
    )
```

profile of v0, /device:TPU:1, one launch (start us, length us, event | category | flops | bytes accessed | tf_op | source)
XLA Modules:
  0.0 404.8 jit_solution(9965831274928698432)
XLA Ops:
  2.5 32.3 %all_gather.6 = bf16[256,512]{1,0:T(8,128)(2,1)} all-gather(bf16[32,512]{1,0:T(8,128)(2,1)} %param.15), channel_id=1, replica_groups=mesh['seq'=16,'head'=8] {'head'}, dimensions={0}, use_global_device_ids=true | all-gather | bytes 294912 | tf_op jit(solution)/shard_map/all_gather | solution.py:24
  34.8 2.3 copy.35
  37.1 28.5 %all_gather.7 = bf16[256,64]{1,0:T(8,128)(2,1)S(1)} all-gather(bf16[32,64]{1,0:T(8,128)(2,1)} %param.16), channel_id=1, replica_groups=mesh['seq'=16,'head'=8] {'head'}, dimensions={0}, use_global_device_ids=true | all-gather | bytes 36864 | tf_op jit(solution)/shard_map/all_gather | solution.py:25
  67.6 13.5 %conditional.2 = (f32[16,256]{1,0:T(8,128)}, f32[16,256]{1,0:T(8,128)S(1)}, f32[16,256,128]{2,1,0:T(8,128)S(1)}) conditional(s32[]{:T(128)} %convert_element_type.34, () %tuple.28, (s32[256]{0:T(256)}, bf16[256,512]{1,0:T(8,128)(2,1)}, bf16[512,2048]{1,0:T(8,128)(2,1)}, bf16[256,16,128]{0,2,1:T(8,128)(2,1)}, bf16[256,64]{1,0:T(8,128)(2,1)S(1)}, ...), branch_computations={%region_2.0_spmd, %region_3.6_spmd} | conditional | flops 1756971008 | bytes 42423376 | solution.py:63
  67.6 2.4 fusion.12
  78.6 2.4 fusion.9
  83.6 319.8 %while.21 = (s32[]{:T(128)}, f32[16,256]{1,0:T(8,128)}, f32[16,256]{1,0:T(8,128)S(1)}, f32[16,256,128]{2,1,0:T(8,128)S(1)}, bf16[256,512]{1,0:T(8,128)(2,1)}, /*...) while((s32[]{:T(128)}, f32[16,256]{1,0:T(8,128)}, ...), condition=%wide.region_12.13_spmd, body=%wide.region_6.12_spmd.sunk | while | flops 1757487360 | bytes 46376392 | solution.py:78
  83.6 13.6 %collective-permute-start.1 = (bf16[256,512]{1,0:T(8,128)(2,1)}, bf16[256,512]{1,0:T(8,128)(2,1)S(1)}, u32[]{:S(2)}, u32[]{:S(2)}) collective-permute-start(bf16[256,512]{1,0:T(8,128)(2,1)} %get-tuple-element.384), channel_id=1, source_target_pairs={{120,0},{0,8},{8,16},{16,24},{24,32},{32,40},{40,48},{48,56},{56,6... | collective-permute-start | bytes 786440 | tf_op jit(solution)/shard_map/while/body/eval_jaxpr/ppermute | solution.py:14
  98.8 2.3 collective-permute-done
  103.0 10.8 %conditional.4 = ((f32[16,256]{1,0:T(8,128)}, f32[16,256]{1,0:T(8,128)S(1)}, f32[16,256,128]{2,1,0:T(8,128)S(1)})) conditional(s32[]{:T(128)} %convert_element_type.63, (f32[16,256]{1,0:T(8,128)}, f32[16,256]{1,0:T(8,128)S(1)}, f32[16,256,128]{2,1,0:T(8,128)S(1)}) %tuple.50, (s32[256]{0:T(256)S(1)}, s32[256]{0:T(256)S(1)}, ...), branch_computations={%region_8.8_spmd, %region_9.11_spmd} | conditional | flops 1757487104 | bytes 44599356 | solution.py:63
  103.0 2.3 fusion.33
  114.5 2.5 collective-permute-start.1
  117.1 2.5 collective-permute-start
  122.8 10.8 %conditional.4 = ((f32[16,256]{1,0:T(8,128)}, f32[16,256]{1,0:T(8,128)S(1)}, f32[16,256,128]{2,1,0:T(8,128)S(1)})) conditional(s32[]{:T(128)} %convert_element_type.63, (f32[16,256]{1,0:T(8,128)}, f32[16,256]{1,0:T(8,128)S(1)}, f32[16,256,128]{2,1,0:T(8,128)S(1)}) %tuple.50, (s32[256]{0:T(256)S(1)}, s32[256]{0:T(256)S(1)}, ...), branch_computations={%region_8.8_spmd, %region_9.11_spmd} | conditional | flops 1757487104 | bytes 44599356 | solution.py:63
  122.8 2.3 fusion.33
  134.4 2.5 collective-permute-start.1
  136.9 3.4 collective-permute-start
  142.9 10.8 %conditional.4 = ((f32[16,256]{1,0:T(8,128)}, f32[16,256]{1,0:T(8,128)S(1)}, f32[16,256,128]{2,1,0:T(8,128)S(1)})) conditional(s32[]{:T(128)} %convert_element_type.63, (f32[16,256]{1,0:T(8,128)}, f32[16,256]{1,0:T(8,128)S(1)}, f32[16,256,128]{2,1,0:T(8,128)S(1)}) %tuple.50, (s32[256]{0:T(256)S(1)}, s32[256]{0:T(256)S(1)}, ...), branch_computations={%region_8.8_spmd, %region_9.11_spmd} | conditional | flops 1757487104 | bytes 44599356 | solution.py:63
  142.9 2.3 fusion.33
  154.4 3.2 collective-permute-start.2
  157.6 3.4 collective-permute-start
  163.6 10.8 %conditional.4 = ((f32[16,256]{1,0:T(8,128)}, f32[16,256]{1,0:T(8,128)S(1)}, f32[16,256,128]{2,1,0:T(8,128)S(1)})) conditional(s32[]{:T(128)} %convert_element_type.63, (f32[16,256]{1,0:T(8,128)}, f32[16,256]{1,0:T(8,128)S(1)}, f32[16,256,128]{2,1,0:T(8,128)S(1)}) %tuple.50, (s32[256]{0:T(256)S(1)}, s32[256]{0:T(256)S(1)}, ...), branch_computations={%region_8.8_spmd, %region_9.11_spmd} | conditional | flops 1757487104 | bytes 44599356 | solution.py:63
  163.6 2.3 fusion.33
  175.2 2.3 collective-permute-start.1
  178.3 3.4 collective-permute-start
  184.3 10.8 %conditional.4 = ((f32[16,256]{1,0:T(8,128)}, f32[16,256]{1,0:T(8,128)S(1)}, f32[16,256,128]{2,1,0:T(8,128)S(1)})) conditional(s32[]{:T(128)} %convert_element_type.63, (f32[16,256]{1,0:T(8,128)}, f32[16,256]{1,0:T(8,128)S(1)}, f32[16,256,128]{2,1,0:T(8,128)S(1)}) %tuple.50, (s32[256]{0:T(256)S(1)}, s32[256]{0:T(256)S(1)}, ...), branch_computations={%region_8.8_spmd, %region_9.11_spmd} | conditional | flops 1757487104 | bytes 44599356 | solution.py:63
  184.4 2.3 fusion.33
  195.9 2.3 collective-permute-start.1
  199.1 3.4 collective-permute-start
  205.1 10.8 %conditional.4 = ((f32[16,256]{1,0:T(8,128)}, f32[16,256]{1,0:T(8,128)S(1)}, f32[16,256,128]{2,1,0:T(8,128)S(1)})) conditional(s32[]{:T(128)} %convert_element_type.63, (f32[16,256]{1,0:T(8,128)}, f32[16,256]{1,0:T(8,128)S(1)}, f32[16,256,128]{2,1,0:T(8,128)S(1)}) %tuple.50, (s32[256]{0:T(256)S(1)}, s32[256]{0:T(256)S(1)}, ...), branch_computations={%region_8.8_spmd, %region_9.11_spmd} | conditional | flops 1757487104 | bytes 44599356 | solution.py:63
  205.1 2.3 fusion.33
  216.6 3.2 collective-permute-start.2
  219.8 3.4 collective-permute-start
  225.8 10.8 %conditional.4 = ((f32[16,256]{1,0:T(8,128)}, f32[16,256]{1,0:T(8,128)S(1)}, f32[16,256,128]{2,1,0:T(8,128)S(1)})) conditional(s32[]{:T(128)} %convert_element_type.63, (f32[16,256]{1,0:T(8,128)}, f32[16,256]{1,0:T(8,128)S(1)}, f32[16,256,128]{2,1,0:T(8,128)S(1)}) %tuple.50, (s32[256]{0:T(256)S(1)}, s32[256]{0:T(256)S(1)}, ...), branch_computations={%region_8.8_spmd, %region_9.11_spmd} | conditional | flops 1757487104 | bytes 44599356 | solution.py:63
  225.8 2.3 fusion.33
  237.4 3.2 collective-permute-start.2
  240.6 3.4 collective-permute-start
  246.6 10.8 %conditional.4 = ((f32[16,256]{1,0:T(8,128)}, f32[16,256]{1,0:T(8,128)S(1)}, f32[16,256,128]{2,1,0:T(8,128)S(1)})) conditional(s32[]{:T(128)} %convert_element_type.63, (f32[16,256]{1,0:T(8,128)}, f32[16,256]{1,0:T(8,128)S(1)}, f32[16,256,128]{2,1,0:T(8,128)S(1)}) %tuple.50, (s32[256]{0:T(256)S(1)}, s32[256]{0:T(256)S(1)}, ...), branch_computations={%region_8.8_spmd, %region_9.11_spmd} | conditional | flops 1757487104 | bytes 44599356 | solution.py:63
  246.6 2.3 fusion.33
  258.1 3.2 collective-permute-start.2
  261.3 3.4 collective-permute-start
  267.3 10.8 %conditional.4 = ((f32[16,256]{1,0:T(8,128)}, f32[16,256]{1,0:T(8,128)S(1)}, f32[16,256,128]{2,1,0:T(8,128)S(1)})) conditional(s32[]{:T(128)} %convert_element_type.63, (f32[16,256]{1,0:T(8,128)}, f32[16,256]{1,0:T(8,128)S(1)}, f32[16,256,128]{2,1,0:T(8,128)S(1)}) %tuple.50, (s32[256]{0:T(256)S(1)}, s32[256]{0:T(256)S(1)}, ...), branch_computations={%region_8.8_spmd, %region_9.11_spmd} | conditional | flops 1757487104 | bytes 44599356 | solution.py:63
  267.3 2.3 fusion.33
  278.9 2.3 collective-permute-start.1
  282.1 3.4 collective-permute-start
  288.1 10.8 %conditional.4 = ((f32[16,256]{1,0:T(8,128)}, f32[16,256]{1,0:T(8,128)S(1)}, f32[16,256,128]{2,1,0:T(8,128)S(1)})) conditional(s32[]{:T(128)} %convert_element_type.63, (f32[16,256]{1,0:T(8,128)}, f32[16,256]{1,0:T(8,128)S(1)}, f32[16,256,128]{2,1,0:T(8,128)S(1)}) %tuple.50, (s32[256]{0:T(256)S(1)}, s32[256]{0:T(256)S(1)}, ...), branch_computations={%region_8.8_spmd, %region_9.11_spmd} | conditional | flops 1757487104 | bytes 44599356 | solution.py:63
  288.1 2.3 fusion.33
  299.6 2.3 collective-permute-start.1
  302.8 3.4 collective-permute-start
  309.5 13.1 %collective-permute-start.1 = (bf16[256,512]{1,0:T(8,128)(2,1)}, bf16[256,512]{1,0:T(8,128)(2,1)S(1)}, u32[]{:S(2)}, u32[]{:S(2)}) collective-permute-start(bf16[256,512]{1,0:T(8,128)(2,1)} %get-tuple-element.384), channel_id=1, source_target_pairs={{120,0},{0,8},{8,16},{16,24},{24,32},{32,40},{40,48},{48,56},{56,6... | collective-permute-start | bytes 786440 | tf_op jit(solution)/shard_map/while/body/eval_jaxpr/ppermute | solution.py:14
  323.5 3.4 collective-permute-start
  329.5 10.8 %conditional.4 = ((f32[16,256]{1,0:T(8,128)}, f32[16,256]{1,0:T(8,128)S(1)}, f32[16,256,128]{2,1,0:T(8,128)S(1)})) conditional(s32[]{:T(128)} %convert_element_type.63, (f32[16,256]{1,0:T(8,128)}, f32[16,256]{1,0:T(8,128)S(1)}, f32[16,256,128]{2,1,0:T(8,128)S(1)}) %tuple.50, (s32[256]{0:T(256)S(1)}, s32[256]{0:T(256)S(1)}, ...), branch_computations={%region_8.8_spmd, %region_9.11_spmd} | conditional | flops 1757487104 | bytes 44599356 | solution.py:63
  329.6 2.3 fusion.33
  341.1 3.2 collective-permute-start.2
  344.3 3.4 collective-permute-start
  350.3 10.8 %conditional.4 = ((f32[16,256]{1,0:T(8,128)}, f32[16,256]{1,0:T(8,128)S(1)}, f32[16,256,128]{2,1,0:T(8,128)S(1)})) conditional(s32[]{:T(128)} %convert_element_type.63, (f32[16,256]{1,0:T(8,128)}, f32[16,256]{1,0:T(8,128)S(1)}, f32[16,256,128]{2,1,0:T(8,128)S(1)}) %tuple.50, (s32[256]{0:T(256)S(1)}, s32[256]{0:T(256)S(1)}, ...), branch_computations={%region_8.8_spmd, %region_9.11_spmd} | conditional | flops 1757487104 | bytes 44599356 | solution.py:63
  350.3 2.3 fusion.33
  361.8 2.3 collective-permute-start.1
  364.1 4.3 %collective-permute-start = (s32[256]{0:T(256)S(1)}, s32[256]{0:T(256)S(1)}, u32[]{:S(2)}, u32[]{:S(2)}) collective-permute-start(s32[256]{0:T(256)S(1)} %get-tuple-element.386), channel_id=1, source_target_pairs={{120,0},{0,8},{8,16},{16,24},{24,32},{32,40},{40,48},{48,56},{56,6... | collective-permute-start | bytes 3080 | tf_op jit(solution)/shard_map/while/body/eval_jaxpr/ppermute | solution.py:14
  371.7 2.3 collective-permute-start.1
  374.0 11.7 %collective-permute-start.2 = (bf16[256,64]{0,1:T(8,128)(2,1)S(1)}, bf16[256,64]{0,1:T(8,128)(2,1)S(1)}, u32[]{:S(2)}, u32[]{:S(2)}) collective-permute-start(bf16[256,64]{0,1:T(8,128)(2,1)S(1)} %get-tuple-element.385), channel_id=1, source_target_pairs={{120,0},{0,8},{8,16},{16,24},{24,32},{32,40},{40,48},{48,56},{56,6... | collective-permute-start | bytes 98312 | tf_op jit(solution)/shard_map/while/body/eval_jaxpr/ppermute | solution.py:14
  385.8 3.4 collective-permute-start
  391.8 10.8 %conditional.4 = ((f32[16,256]{1,0:T(8,128)}, f32[16,256]{1,0:T(8,128)S(1)}, f32[16,256,128]{2,1,0:T(8,128)S(1)})) conditional(s32[]{:T(128)} %convert_element_type.63, (f32[16,256]{1,0:T(8,128)}, f32[16,256]{1,0:T(8,128)S(1)}, f32[16,256,128]{2,1,0:T(8,128)S(1)}) %tuple.50, (s32[256]{0:T(256)S(1)}, s32[256]{0:T(256)S(1)}, ...), branch_computations={%region_8.8_spmd, %region_9.11_spmd} | conditional | flops 1757487104 | bytes 44599356 | solution.py:63
  391.8 2.3 fusion.33
  (283 shorter events, 163.1 us)
Async XLA Ops:
  67.6 15.9 %copy-start.2 = (s32[256]{0:T(256)S(1)}, s32[256]{0:T(256)}, u32[]{:S(2)}) copy-start(s32[256]{0:T(256)} %param.17) | copy-start | bytes 3076
  67.6 4.4 %copy-start.3 = (s32[256]{0:T(256)S(1)}, s32[256]{0:T(256)}, u32[]{:S(2)}) copy-start(s32[256]{0:T(256)} %get-tuple-element.147) | copy-start | bytes 3076 | tf_op jit(solution)/shard_map/cond
  74.1 2.8 copy-start
  83.6 19.4 %collective-permute-start.1 = (bf16[256,512]{1,0:T(8,128)(2,1)}, bf16[256,512]{1,0:T(8,128)(2,1)S(1)}, u32[]{:S(2)}, u32[]{:S(2)}) collective-permute-start(bf16[256,512]{1,0:T(8,128)(2,1)} %get-tuple-element.384), channel_id=1, source_target_pairs={{120,0},{0,8},{8,16},{16,24},{24,32},{32,40},{40,48},{48,56},{56,6... | collective-permute-start | bytes 786440 | tf_op jit(solution)/shard_map/while/body/eval_jaxpr/ppermute | solution.py:14
  97.2 5.8 %collective-permute-start.2 = (bf16[256,64]{0,1:T(8,128)(2,1)S(1)}, bf16[256,64]{0,1:T(8,128)(2,1)S(1)}, u32[]{:S(2)}, u32[]{:S(2)}) collective-permute-start(bf16[256,64]{0,1:T(8,128)(2,1)S(1)} %get-tuple-element.385), channel_id=1, source_target_pairs={{120,0},{0,8},{8,16},{16,24},{24,32},{32,40},{40,48},{48,56},{56,6... | collective-permute-start | bytes 98312 | tf_op jit(solution)/shard_map/while/body/eval_jaxpr/ppermute | solution.py:14
  97.3 3.8 collective-permute-start
  108.2 3.0 copy-start.1
  114.5 8.3 %collective-permute-start.1 = (bf16[256,512]{1,0:T(8,128)(2,1)}, bf16[256,512]{1,0:T(8,128)(2,1)S(1)}, u32[]{:S(2)}, u32[]{:S(2)}) collective-permute-start(bf16[256,512]{1,0:T(8,128)(2,1)} %get-tuple-element.384), channel_id=1, source_target_pairs={{120,0},{0,8},{8,16},{16,24},{24,32},{32,40},{40,48},{48,56},{56,6... | collective-permute-start | bytes 786440 | tf_op jit(solution)/shard_map/while/body/eval_jaxpr/ppermute | solution.py:14
  117.0 5.8 %collective-permute-start.2 = (bf16[256,64]{0,1:T(8,128)(2,1)S(1)}, bf16[256,64]{0,1:T(8,128)(2,1)S(1)}, u32[]{:S(2)}, u32[]{:S(2)}) collective-permute-start(bf16[256,64]{0,1:T(8,128)(2,1)S(1)} %get-tuple-element.385), channel_id=1, source_target_pairs={{120,0},{0,8},{8,16},{16,24},{24,32},{32,40},{40,48},{48,56},{56,6... | collective-permute-start | bytes 98312 | tf_op jit(solution)/shard_map/while/body/eval_jaxpr/ppermute | solution.py:14
  117.1 3.9 collective-permute-start
  128.1 3.0 copy-start.1
  134.4 8.5 %collective-permute-start.1 = (bf16[256,512]{1,0:T(8,128)(2,1)}, bf16[256,512]{1,0:T(8,128)(2,1)S(1)}, u32[]{:S(2)}, u32[]{:S(2)}) collective-permute-start(bf16[256,512]{1,0:T(8,128)(2,1)} %get-tuple-element.384), channel_id=1, source_target_pairs={{120,0},{0,8},{8,16},{16,24},{24,32},{32,40},{40,48},{48,56},{56,6... | collective-permute-start | bytes 786440 | tf_op jit(solution)/shard_map/while/body/eval_jaxpr/ppermute | solution.py:14
  136.9 6.0 %collective-permute-start.2 = (bf16[256,64]{0,1:T(8,128)(2,1)S(1)}, bf16[256,64]{0,1:T(8,128)(2,1)S(1)}, u32[]{:S(2)}, u32[]{:S(2)}) collective-permute-start(bf16[256,64]{0,1:T(8,128)(2,1)S(1)} %get-tuple-element.385), channel_id=1, source_target_pairs={{120,0},{0,8},{8,16},{16,24},{24,32},{32,40},{40,48},{48,56},{56,6... | collective-permute-start | bytes 98312 | tf_op jit(solution)/shard_map/while/body/eval_jaxpr/ppermute | solution.py:14
  136.9 4.1 %collective-permute-start = (s32[256]{0:T(256)S(1)}, s32[256]{0:T(256)S(1)}, u32[]{:S(2)}, u32[]{:S(2)}) collective-permute-start(s32[256]{0:T(256)S(1)} %get-tuple-element.386), channel_id=1, source_target_pairs={{120,0},{0,8},{8,16},{16,24},{24,32},{32,40},{40,48},{48,56},{56,6... | collective-permute-start | bytes 3080 | tf_op jit(solution)/shard_map/while/body/eval_jaxpr/ppermute | solution.py:14
  148.1 3.0 copy-start.1
  154.4 9.2 %collective-permute-start.1 = (bf16[256,512]{1,0:T(8,128)(2,1)}, bf16[256,512]{1,0:T(8,128)(2,1)S(1)}, u32[]{:S(2)}, u32[]{:S(2)}) collective-permute-start(bf16[256,512]{1,0:T(8,128)(2,1)} %get-tuple-element.384), channel_id=1, source_target_pairs={{120,0},{0,8},{8,16},{16,24},{24,32},{32,40},{40,48},{48,56},{56,6... | collective-permute-start | bytes 786440 | tf_op jit(solution)/shard_map/while/body/eval_jaxpr/ppermute | solution.py:14
  154.4 9.1 %collective-permute-start.2 = (bf16[256,64]{0,1:T(8,128)(2,1)S(1)}, bf16[256,64]{0,1:T(8,128)(2,1)S(1)}, u32[]{:S(2)}, u32[]{:S(2)}) collective-permute-start(bf16[256,64]{0,1:T(8,128)(2,1)S(1)} %get-tuple-element.385), channel_id=1, source_target_pairs={{120,0},{0,8},{8,16},{16,24},{24,32},{32,40},{40,48},{48,56},{56,6... | collective-permute-start | bytes 98312 | tf_op jit(solution)/shard_map/while/body/eval_jaxpr/ppermute | solution.py:14
  157.6 4.1 %collective-permute-start = (s32[256]{0:T(256)S(1)}, s32[256]{0:T(256)S(1)}, u32[]{:S(2)}, u32[]{:S(2)}) collective-permute-start(s32[256]{0:T(256)S(1)} %get-tuple-element.386), channel_id=1, source_target_pairs={{120,0},{0,8},{8,16},{16,24},{24,32},{32,40},{40,48},{48,56},{56,6... | collective-permute-start | bytes 3080 | tf_op jit(solution)/shard_map/while/body/eval_jaxpr/ppermute | solution.py:14
  168.9 3.0 copy-start.1
  175.2 9.2 %collective-permute-start.1 = (bf16[256,512]{1,0:T(8,128)(2,1)}, bf16[256,512]{1,0:T(8,128)(2,1)S(1)}, u32[]{:S(2)}, u32[]{:S(2)}) collective-permute-start(bf16[256,512]{1,0:T(8,128)(2,1)} %get-tuple-element.384), channel_id=1, source_target_pairs={{120,0},{0,8},{8,16},{16,24},{24,32},{32,40},{40,48},{48,56},{56,6... | collective-permute-start | bytes 786440 | tf_op jit(solution)/shard_map/while/body/eval_jaxpr/ppermute | solution.py:14
  177.4 6.9 %collective-permute-start.2 = (bf16[256,64]{0,1:T(8,128)(2,1)S(1)}, bf16[256,64]{0,1:T(8,128)(2,1)S(1)}, u32[]{:S(2)}, u32[]{:S(2)}) collective-permute-start(bf16[256,64]{0,1:T(8,128)(2,1)S(1)} %get-tuple-element.385), channel_id=1, source_target_pairs={{120,0},{0,8},{8,16},{16,24},{24,32},{32,40},{40,48},{48,56},{56,6... | collective-permute-start | bytes 98312 | tf_op jit(solution)/shard_map/while/body/eval_jaxpr/ppermute | solution.py:14
  178.3 4.1 %collective-permute-start = (s32[256]{0:T(256)S(1)}, s32[256]{0:T(256)S(1)}, u32[]{:S(2)}, u32[]{:S(2)}) collective-permute-start(s32[256]{0:T(256)S(1)} %get-tuple-element.386), channel_id=1, source_target_pairs={{120,0},{0,8},{8,16},{16,24},{24,32},{32,40},{40,48},{48,56},{56,6... | collective-permute-start | bytes 3080 | tf_op jit(solution)/shard_map/while/body/eval_jaxpr/ppermute | solution.py:14
  189.6 3.0 copy-start.1
  195.9 9.2 %collective-permute-start.1 = (bf16[256,512]{1,0:T(8,128)(2,1)}, bf16[256,512]{1,0:T(8,128)(2,1)S(1)}, u32[]{:S(2)}, u32[]{:S(2)}) collective-permute-start(bf16[256,512]{1,0:T(8,128)(2,1)} %get-tuple-element.384), channel_id=1, source_target_pairs={{120,0},{0,8},{8,16},{16,24},{24,32},{32,40},{40,48},{48,56},{56,6... | collective-permute-start | bytes 786440 | tf_op jit(solution)/shard_map/while/body/eval_jaxpr/ppermute | solution.py:14
  198.2 6.9 %collective-permute-start.2 = (bf16[256,64]{0,1:T(8,128)(2,1)S(1)}, bf16[256,64]{0,1:T(8,128)(2,1)S(1)}, u32[]{:S(2)}, u32[]{:S(2)}) collective-permute-start(bf16[256,64]{0,1:T(8,128)(2,1)S(1)} %get-tuple-element.385), channel_id=1, source_target_pairs={{120,0},{0,8},{8,16},{16,24},{24,32},{32,40},{40,48},{48,56},{56,6... | collective-permute-start | bytes 98312 | tf_op jit(solution)/shard_map/while/body/eval_jaxpr/ppermute | solution.py:14
  199.1 4.1 %collective-permute-start = (s32[256]{0:T(256)S(1)}, s32[256]{0:T(256)S(1)}, u32[]{:S(2)}, u32[]{:S(2)}) collective-permute-start(s32[256]{0:T(256)S(1)} %get-tuple-element.386), channel_id=1, source_target_pairs={{120,0},{0,8},{8,16},{16,24},{24,32},{32,40},{40,48},{48,56},{56,6... | collective-permute-start | bytes 3080 | tf_op jit(solution)/shard_map/while/body/eval_jaxpr/ppermute | solution.py:14
  210.3 3.0 copy-start.1
  216.6 9.2 %collective-permute-start.1 = (bf16[256,512]{1,0:T(8,128)(2,1)}, bf16[256,512]{1,0:T(8,128)(2,1)S(1)}, u32[]{:S(2)}, u32[]{:S(2)}) collective-permute-start(bf16[256,512]{1,0:T(8,128)(2,1)} %get-tuple-element.384), channel_id=1, source_target_pairs={{120,0},{0,8},{8,16},{16,24},{24,32},{32,40},{40,48},{48,56},{56,6... | collective-permute-start | bytes 786440 | tf_op jit(solution)/shard_map/while/body/eval_jaxpr/ppermute | solution.py:14
  216.6 9.1 %collective-permute-start.2 = (bf16[256,64]{0,1:T(8,128)(2,1)S(1)}, bf16[256,64]{0,1:T(8,128)(2,1)S(1)}, u32[]{:S(2)}, u32[]{:S(2)}) collective-permute-start(bf16[256,64]{0,1:T(8,128)(2,1)S(1)} %get-tuple-element.385), channel_id=1, source_target_pairs={{120,0},{0,8},{8,16},{16,24},{24,32},{32,40},{40,48},{48,56},{56,6... | collective-permute-start | bytes 98312 | tf_op jit(solution)/shard_map/while/body/eval_jaxpr/ppermute | solution.py:14
  219.8 4.1 %collective-permute-start = (s32[256]{0:T(256)S(1)}, s32[256]{0:T(256)S(1)}, u32[]{:S(2)}, u32[]{:S(2)}) collective-permute-start(s32[256]{0:T(256)S(1)} %get-tuple-element.386), channel_id=1, source_target_pairs={{120,0},{0,8},{8,16},{16,24},{24,32},{32,40},{40,48},{48,56},{56,6... | collective-permute-start | bytes 3080 | tf_op jit(solution)/shard_map/while/body/eval_jaxpr/ppermute | solution.py:14
  231.1 3.0 copy-start.1
  237.4 9.2 %collective-permute-start.1 = (bf16[256,512]{1,0:T(8,128)(2,1)}, bf16[256,512]{1,0:T(8,128)(2,1)S(1)}, u32[]{:S(2)}, u32[]{:S(2)}) collective-permute-start(bf16[256,512]{1,0:T(8,128)(2,1)} %get-tuple-element.384), channel_id=1, source_target_pairs={{120,0},{0,8},{8,16},{16,24},{24,32},{32,40},{40,48},{48,56},{56,6... | collective-permute-start | bytes 786440 | tf_op jit(solution)/shard_map/while/body/eval_jaxpr/ppermute | solution.py:14
  237.4 9.1 %collective-permute-start.2 = (bf16[256,64]{0,1:T(8,128)(2,1)S(1)}, bf16[256,64]{0,1:T(8,128)(2,1)S(1)}, u32[]{:S(2)}, u32[]{:S(2)}) collective-permute-start(bf16[256,64]{0,1:T(8,128)(2,1)S(1)} %get-tuple-element.385), channel_id=1, source_target_pairs={{120,0},{0,8},{8,16},{16,24},{24,32},{32,40},{40,48},{48,56},{56,6... | collective-permute-start | bytes 98312 | tf_op jit(solution)/shard_map/while/body/eval_jaxpr/ppermute | solution.py:14
  240.6 4.1 %collective-permute-start = (s32[256]{0:T(256)S(1)}, s32[256]{0:T(256)S(1)}, u32[]{:S(2)}, u32[]{:S(2)}) collective-permute-start(s32[256]{0:T(256)S(1)} %get-tuple-element.386), channel_id=1, source_target_pairs={{120,0},{0,8},{8,16},{16,24},{24,32},{32,40},{40,48},{48,56},{56,6... | collective-permute-start | bytes 3080 | tf_op jit(solution)/shard_map/while/body/eval_jaxpr/ppermute | solution.py:14
  251.8 3.0 copy-start.1
  258.1 9.2 %collective-permute-start.1 = (bf16[256,512]{1,0:T(8,128)(2,1)}, bf16[256,512]{1,0:T(8,128)(2,1)S(1)}, u32[]{:S(2)}, u32[]{:S(2)}) collective-permute-start(bf16[256,512]{1,0:T(8,128)(2,1)} %get-tuple-element.384), channel_id=1, source_target_pairs={{120,0},{0,8},{8,16},{16,24},{24,32},{32,40},{40,48},{48,56},{56,6... | collective-permute-start | bytes 786440 | tf_op jit(solution)/shard_map/while/body/eval_jaxpr/ppermute | solution.py:14
  258.1 9.1 %collective-permute-start.2 = (bf16[256,64]{0,1:T(8,128)(2,1)S(1)}, bf16[256,64]{0,1:T(8,128)(2,1)S(1)}, u32[]{:S(2)}, u32[]{:S(2)}) collective-permute-start(bf16[256,64]{0,1:T(8,128)(2,1)S(1)} %get-tuple-element.385), channel_id=1, source_target_pairs={{120,0},{0,8},{8,16},{16,24},{24,32},{32,40},{40,48},{48,56},{56,6... | collective-permute-start | bytes 98312 | tf_op jit(solution)/shard_map/while/body/eval_jaxpr/ppermute | solution.py:14
  261.3 4.1 %collective-permute-start = (s32[256]{0:T(256)S(1)}, s32[256]{0:T(256)S(1)}, u32[]{:S(2)}, u32[]{:S(2)}) collective-permute-start(s32[256]{0:T(256)S(1)} %get-tuple-element.386), channel_id=1, source_target_pairs={{120,0},{0,8},{8,16},{16,24},{24,32},{32,40},{40,48},{48,56},{56,6... | collective-permute-start | bytes 3080 | tf_op jit(solution)/shard_map/while/body/eval_jaxpr/ppermute | solution.py:14
  272.6 3.0 copy-start.1
  278.9 9.2 %collective-permute-start.1 = (bf16[256,512]{1,0:T(8,128)(2,1)}, bf16[256,512]{1,0:T(8,128)(2,1)S(1)}, u32[]{:S(2)}, u32[]{:S(2)}) collective-permute-start(bf16[256,512]{1,0:T(8,128)(2,1)} %get-tuple-element.384), channel_id=1, source_target_pairs={{120,0},{0,8},{8,16},{16,24},{24,32},{32,40},{40,48},{48,56},{56,6... | collective-permute-start | bytes 786440 | tf_op jit(solution)/shard_map/while/body/eval_jaxpr/ppermute | solution.py:14
  281.1 6.9 %collective-permute-start.2 = (bf16[256,64]{0,1:T(8,128)(2,1)S(1)}, bf16[256,64]{0,1:T(8,128)(2,1)S(1)}, u32[]{:S(2)}, u32[]{:S(2)}) collective-permute-start(bf16[256,64]{0,1:T(8,128)(2,1)S(1)} %get-tuple-element.385), channel_id=1, source_target_pairs={{120,0},{0,8},{8,16},{16,24},{24,32},{32,40},{40,48},{48,56},{56,6... | collective-permute-start | bytes 98312 | tf_op jit(solution)/shard_map/while/body/eval_jaxpr/ppermute | solution.py:14
  282.1 4.1 %collective-permute-start = (s32[256]{0:T(256)S(1)}, s32[256]{0:T(256)S(1)}, u32[]{:S(2)}, u32[]{:S(2)}) collective-permute-start(s32[256]{0:T(256)S(1)} %get-tuple-element.386), channel_id=1, source_target_pairs={{120,0},{0,8},{8,16},{16,24},{24,32},{32,40},{40,48},{48,56},{56,6... | collective-permute-start | bytes 3080 | tf_op jit(solution)/shard_map/while/body/eval_jaxpr/ppermute | solution.py:14
  293.3 3.0 copy-start.1
  299.6 9.2 %collective-permute-start.1 = (bf16[256,512]{1,0:T(8,128)(2,1)}, bf16[256,512]{1,0:T(8,128)(2,1)S(1)}, u32[]{:S(2)}, u32[]{:S(2)}) collective-permute-start(bf16[256,512]{1,0:T(8,128)(2,1)} %get-tuple-element.384), channel_id=1, source_target_pairs={{120,0},{0,8},{8,16},{16,24},{24,32},{32,40},{40,48},{48,56},{56,6... | collective-permute-start | bytes 786440 | tf_op jit(solution)/shard_map/while/body/eval_jaxpr/ppermute | solution.py:14
  301.9 6.9 %collective-permute-start.2 = (bf16[256,64]{0,1:T(8,128)(2,1)S(1)}, bf16[256,64]{0,1:T(8,128)(2,1)S(1)}, u32[]{:S(2)}, u32[]{:S(2)}) collective-permute-start(bf16[256,64]{0,1:T(8,128)(2,1)S(1)} %get-tuple-element.385), channel_id=1, source_target_pairs={{120,0},{0,8},{8,16},{16,24},{24,32},{32,40},{40,48},{48,56},{56,6... | collective-permute-start | bytes 98312 | tf_op jit(solution)/shard_map/while/body/eval_jaxpr/ppermute | solution.py:14
  302.8 4.1 %collective-permute-start = (s32[256]{0:T(256)S(1)}, s32[256]{0:T(256)S(1)}, u32[]{:S(2)}, u32[]{:S(2)}) collective-permute-start(s32[256]{0:T(256)S(1)} %get-tuple-element.386), channel_id=1, source_target_pairs={{120,0},{0,8},{8,16},{16,24},{24,32},{32,40},{40,48},{48,56},{56,6... | collective-permute-start | bytes 3080 | tf_op jit(solution)/shard_map/while/body/eval_jaxpr/ppermute | solution.py:14
  309.5 20.0 %collective-permute-start.1 = (bf16[256,512]{1,0:T(8,128)(2,1)}, bf16[256,512]{1,0:T(8,128)(2,1)S(1)}, u32[]{:S(2)}, u32[]{:S(2)}) collective-permute-start(bf16[256,512]{1,0:T(8,128)(2,1)} %get-tuple-element.384), channel_id=1, source_target_pairs={{120,0},{0,8},{8,16},{16,24},{24,32},{32,40},{40,48},{48,56},{56,6... | collective-permute-start | bytes 786440 | tf_op jit(solution)/shard_map/while/body/eval_jaxpr/ppermute | solution.py:14
  322.6 6.9 %collective-permute-start.2 = (bf16[256,64]{0,1:T(8,128)(2,1)S(1)}, bf16[256,64]{0,1:T(8,128)(2,1)S(1)}, u32[]{:S(2)}, u32[]{:S(2)}) collective-permute-start(bf16[256,64]{0,1:T(8,128)(2,1)S(1)} %get-tuple-element.385), channel_id=1, source_target_pairs={{120,0},{0,8},{8,16},{16,24},{24,32},{32,40},{40,48},{48,56},{56,6... | collective-permute-start | bytes 98312 | tf_op jit(solution)/shard_map/while/body/eval_jaxpr/ppermute | solution.py:14
  323.5 4.1 %collective-permute-start = (s32[256]{0:T(256)S(1)}, s32[256]{0:T(256)S(1)}, u32[]{:S(2)}, u32[]{:S(2)}) collective-permute-start(s32[256]{0:T(256)S(1)} %get-tuple-element.386), channel_id=1, source_target_pairs={{120,0},{0,8},{8,16},{16,24},{24,32},{32,40},{40,48},{48,56},{56,6... | collective-permute-start | bytes 3080 | tf_op jit(solution)/shard_map/while/body/eval_jaxpr/ppermute | solution.py:14
  334.8 3.0 copy-start.1
  341.1 9.2 %collective-permute-start.1 = (bf16[256,512]{1,0:T(8,128)(2,1)}, bf16[256,512]{1,0:T(8,128)(2,1)S(1)}, u32[]{:S(2)}, u32[]{:S(2)}) collective-permute-start(bf16[256,512]{1,0:T(8,128)(2,1)} %get-tuple-element.384), channel_id=1, source_target_pairs={{120,0},{0,8},{8,16},{16,24},{24,32},{32,40},{40,48},{48,56},{56,6... | collective-permute-start | bytes 786440 | tf_op jit(solution)/shard_map/while/body/eval_jaxpr/ppermute | solution.py:14
  341.1 9.1 %collective-permute-start.2 = (bf16[256,64]{0,1:T(8,128)(2,1)S(1)}, bf16[256,64]{0,1:T(8,128)(2,1)S(1)}, u32[]{:S(2)}, u32[]{:S(2)}) collective-permute-start(bf16[256,64]{0,1:T(8,128)(2,1)S(1)} %get-tuple-element.385), channel_id=1, source_target_pairs={{120,0},{0,8},{8,16},{16,24},{24,32},{32,40},{40,48},{48,56},{56,6... | collective-permute-start | bytes 98312 | tf_op jit(solution)/shard_map/while/body/eval_jaxpr/ppermute | solution.py:14
  344.3 4.1 %collective-permute-start = (s32[256]{0:T(256)S(1)}, s32[256]{0:T(256)S(1)}, u32[]{:S(2)}, u32[]{:S(2)}) collective-permute-start(s32[256]{0:T(256)S(1)} %get-tuple-element.386), channel_id=1, source_target_pairs={{120,0},{0,8},{8,16},{16,24},{24,32},{32,40},{40,48},{48,56},{56,6... | collective-permute-start | bytes 3080 | tf_op jit(solution)/shard_map/while/body/eval_jaxpr/ppermute | solution.py:14
  355.5 3.0 copy-start.1
  361.8 9.2 %collective-permute-start.1 = (bf16[256,512]{1,0:T(8,128)(2,1)}, bf16[256,512]{1,0:T(8,128)(2,1)S(1)}, u32[]{:S(2)}, u32[]{:S(2)}) collective-permute-start(bf16[256,512]{1,0:T(8,128)(2,1)} %get-tuple-element.384), channel_id=1, source_target_pairs={{120,0},{0,8},{8,16},{16,24},{24,32},{32,40},{40,48},{48,56},{56,6... | collective-permute-start | bytes 786440 | tf_op jit(solution)/shard_map/while/body/eval_jaxpr/ppermute | solution.py:14
  364.1 6.9 %collective-permute-start.2 = (bf16[256,64]{0,1:T(8,128)(2,1)S(1)}, bf16[256,64]{0,1:T(8,128)(2,1)S(1)}, u32[]{:S(2)}, u32[]{:S(2)}) collective-permute-start(bf16[256,64]{0,1:T(8,128)(2,1)S(1)} %get-tuple-element.385), channel_id=1, source_target_pairs={{120,0},{0,8},{8,16},{16,24},{24,32},{32,40},{40,48},{48,56},{56,6... | collective-permute-start | bytes 98312 | tf_op jit(solution)/shard_map/while/body/eval_jaxpr/ppermute | solution.py:14
  364.1 5.0 %collective-permute-start = (s32[256]{0:T(256)S(1)}, s32[256]{0:T(256)S(1)}, u32[]{:S(2)}, u32[]{:S(2)}) collective-permute-start(s32[256]{0:T(256)S(1)} %get-tuple-element.386), channel_id=1, source_target_pairs={{120,0},{0,8},{8,16},{16,24},{24,32},{32,40},{40,48},{48,56},{56,6... | collective-permute-start | bytes 3080 | tf_op jit(solution)/shard_map/while/body/eval_jaxpr/ppermute | solution.py:14
  371.7 20.0 %collective-permute-start.1 = (bf16[256,512]{1,0:T(8,128)(2,1)}, bf16[256,512]{1,0:T(8,128)(2,1)S(1)}, u32[]{:S(2)}, u32[]{:S(2)}) collective-permute-start(bf16[256,512]{1,0:T(8,128)(2,1)} %get-tuple-element.384), channel_id=1, source_target_pairs={{120,0},{0,8},{8,16},{16,24},{24,32},{32,40},{40,48},{48,56},{56,6... | collective-permute-start | bytes 786440 | tf_op jit(solution)/shard_map/while/body/eval_jaxpr/ppermute | solution.py:14
  374.0 17.7 %collective-permute-start.2 = (bf16[256,64]{0,1:T(8,128)(2,1)S(1)}, bf16[256,64]{0,1:T(8,128)(2,1)S(1)}, u32[]{:S(2)}, u32[]{:S(2)}) collective-permute-start(bf16[256,64]{0,1:T(8,128)(2,1)S(1)} %get-tuple-element.385), channel_id=1, source_target_pairs={{120,0},{0,8},{8,16},{16,24},{24,32},{32,40},{40,48},{48,56},{56,6... | collective-permute-start | bytes 98312 | tf_op jit(solution)/shard_map/while/body/eval_jaxpr/ppermute | solution.py:14
  385.8 4.1 %collective-permute-start = (s32[256]{0:T(256)S(1)}, s32[256]{0:T(256)S(1)}, u32[]{:S(2)}, u32[]{:S(2)}) collective-permute-start(s32[256]{0:T(256)S(1)} %get-tuple-element.386), channel_id=1, source_target_pairs={{120,0},{0,8},{8,16},{16,24},{24,32},{32,40},{40,48},{48,56},{56,6... | collective-permute-start | bytes 3080 | tf_op jit(solution)/shard_map/while/body/eval_jaxpr/ppermute | solution.py:14
  397.0 3.0 copy-start.1
where the time goes:
time: 411 us; the launch traced here: 405 us
  starting transfers between devices  127 us (31%)
  matrix products  111 us (27%)
  blocking collectives  60.8 us (15%)
  other arithmetic  46.9 us (11%)
  local copies, waits for them, and re-layouts  25.2 us (6%)
  loops' own time  19.9 us (5%)
  waiting for transfers between devices  13.2 us (3%)
    ppermute x45, starting transfers between devices, from_behind(): return lax.ppermute(block, axis, route)  127 us
    dot_general x14, matrix products, compute(): jnp.dot(lat_rows, w_uk, preferred_element_type=jnp.float32)  32.4 us
    all_gather x1, blocking collectives, per_device(): lax.all_gather(latent, 'head', axis=0, tiled=True)  32.3 us
    dot_general x14, matrix products, compute(): jnp.einsum('qhd,kd->hqk', query_rot, rot_rows, preferred_element_type=jnp...  29.1 us
    all_gather x1, blocking collectives, per_device(): lax.all_gather(k_rope, 'head', axis=0, tiled=True)  28.5 us
    dot_general x14, matrix products, compute(): jnp.einsum('hqk,khd->hqd', weights.astype(jnp.bfloat16), values, preferre...  26.8 us
    another operation x1, loops' own time, per_device(): lax.fori_loop(0, cycle_len - 1, cycle_turn, (state, own_block))  18.7 us
    ppermute x45, waiting for transfers between devices, from_behind(): return lax.ppermute(block, axis, route)  13.2 us
  transfers between devices with their start and end apart: 45, of which 15 were waited for; matrix products, arithmetic and copies ran while one was open for 2% of the time, Pallas kernels for 0%

commit v1 on v0

v1 whole, which is shorter than its diff:
```python
import functools
import math

import jax
import jax.numpy as jnp
from jax import lax
from jax.experimental import pallas as pl
from jax.experimental.pallas import tpu as pltpu
from jax.sharding import PartitionSpec as P

MESH = pl.DeviceIdType.MESH
F32 = jnp.float32
BF16 = jnp.bfloat16
NT = (((1,), (1,)), ((), ()))
NOPE = 128
ROPE = 64
LATENT = 512
WIDE = 640
ROWS = 256
CHUNK = 512
UNIT = 32
HEADS = 8
COLS = HEADS * NOPE
SCALE2 = (NOPE + ROPE) ** (-0.5) * math.log2(math.e)
MASKED = -1e30
SLACK = 60.0


def at_rows(start, size, step):
    return pl.ds(pl.multiple_of(start, step), size)


def block_lanes(shape, block, later):
    lane = lax.broadcasted_iota(jnp.int32, shape, 1) - ROPE
    if later:
        return jnp.where((lane > block) & (lane < 32), MASKED, 0.0)
    return jnp.where(lane == block, 1.0, 0.0)


def query_mask(pos_ref):
    top = block_lanes((128, 128), pos_ref[0] // 128, True)
    low = block_lanes((128, 128), pos_ref[128] // 128, True)
    return jnp.concatenate([top, low], 0).astype(BF16)


def gather_attend(
    pos_ref, lat_ref, rot_ref, qn_hbm, qr_hbm, wk_hbm, wv_hbm,
    out_hbm, all_hbm, peak_ref,
    unit, lat, wk, wv, wvt, qn, qr, qmask, qrot, tri, acc, total, shift, done, peak,
    loc_sem, q_send, q_recv, h_send, h_recv, f_send, f_recv, x_send, x_recv, z_send, z_recv,
    d_send, d_recv, o_loc, o_send, o_recv, all_sem,
):
    seq = lax.axis_index("seq")
    head = lax.axis_index("head")
    x, zl, core = seq // 4, (seq // 2) % 2, seq % 2
    y, zh = head // 2, head % 2
    z = zh * 2 + zl
    other = 1 - core

    def seq_at(px, pzl, pc):
        return px * 4 + pzl * 2 + pc

    def chip_x(d):
        return (seq_at((x + d) % 4, zl, core), head)

    def chip_z(d):
        pz = (z + d) % 4
        return (seq_at(x, pz % 2, core), y * 2 + pz // 2)

    def chip_h(d):
        return (seq, (head + d) % 8)

    sibling = (seq_at(x, zl, other), head)
    partners = [chip_h(d) for d in range(1, 8)] + [chip_x(1), chip_x(3), chip_x(2), chip_z(1), chip_z(3), sibling]

    barrier = pltpu.get_barrier_semaphore()
    for p in partners:
        pl.semaphore_signal(barrier, inc=1, device_id=p, device_id_type=MESH)

    mine = at_rows(core * ROWS, ROWS, ROWS)
    mine_cols = at_rows(core * COLS, COLS, COLS)
    their_cols = at_rows(other * COLS, COLS, COLS)
    half_cols = COLS // 2
    local = [
        pltpu.make_async_copy(wv_hbm.at[:, mine_cols], wv, loc_sem.at[0]),
        pltpu.make_async_copy(wk_hbm.at[:, mine_cols], wk, loc_sem.at[1]),
        pltpu.make_async_copy(qn_hbm.at[:, mine_cols], qn.at[mine], loc_sem.at[2]),
        pltpu.make_async_copy(
            qr_hbm.at[:, at_rows(core * half_cols, half_cols, half_cols)], qr.at[mine], loc_sem.at[3]
        ),
    ]
    for c in local:
        c.start()

    unit[:, :LATENT] = lat_ref[...]
    block = jnp.where(head < 4, pos_ref[0] // 128, pos_ref[128] // 128)
    lane = lax.broadcasted_iota(jnp.int32, (UNIT, 128), 1)
    rot = jnp.concatenate([rot_ref[...].astype(F32), jnp.zeros((UNIT, ROPE), F32)], 1)
    unit[:, LATENT:] = jnp.where(lane < ROPE, rot, block_lanes((UNIT, 128), block, False)).astype(BF16)
    qmask[mine] = query_mask(pos_ref)
    own_unit = at_rows(seq * ROWS + head * UNIT, UNIT, UNIT)
    lat[own_unit, :] = unit[...]

    pl.semaphore_wait(barrier, len(partners))

    def remote(src, dst, send, recv, to):
        return pltpu.make_async_remote_copy(
            src_ref=src, dst_ref=dst, send_sem=send, recv_sem=recv, device_id=to, device_id_type=MESH
        )

    def unit_rows(d):
        return lat.at[at_rows(seq * ROWS + ((head + 8 - d) % 8) * UNIT, UNIT, UNIT)]

    def spread(d):
        return remote(unit, lat.at[own_unit], h_send.at[d], h_recv.at[d], chip_h(d))

    def forward_unit(d):
        src = unit_rows(d)
        return remote(src, src, f_send.at[d], f_recv.at[d], sibling)

    def forward_in(d):
        dst = lat.at[at_rows(seq_at(x, zl, other) * ROWS + ((head + 8 - d) % 8) * UNIT, UNIT, UNIT)]
        return remote(dst, dst, f_send.at[d], f_recv.at[d], sibling)

    for d in (4, 2, 6, 1, 7, 3, 5):
        spread(d).start()
    swap = [
        remote(qn_hbm.at[:, their_cols], qn.at[mine], q_send.at[0], q_recv.at[0], sibling),
        remote(
            qr_hbm.at[:, at_rows(other * half_cols, half_cols, half_cols)], qr.at[mine],
            q_send.at[1], q_recv.at[1], sibling,
        ),
        remote(qmask.at[mine], qmask.at[mine], q_send.at[2], q_recv.at[2], sibling),
    ]
    for c in swap:
        c.start()
    theirs = at_rows(other * ROWS, ROWS, ROWS)
    swap_in = [
        remote(qn.at[theirs], qn.at[theirs], q_send.at[0], q_recv.at[0], sibling),
        remote(qr.at[theirs], qr.at[theirs], q_send.at[1], q_recv.at[1], sibling),
        remote(qmask.at[theirs], qmask.at[theirs], q_send.at[2], q_recv.at[2], sibling),
    ]
    forward_unit(0).start()

    key = lax.broadcasted_iota(jnp.int32, (128, 128), 0)
    query = lax.broadcasted_iota(jnp.int32, (128, 128), 1)
    tri[...] = jnp.where(key > query, MASKED, 0.0)
    acc[...] = jnp.zeros_like(acc)
    total[...] = jnp.zeros_like(total)
    local[0].wait()
    for i in range(HEADS):
        wvt[i * 128 : (i + 1) * 128, :] = wv[:, i * 128 : (i + 1) * 128].T
    for c in local[1:]:
        c.wait()
    for c in swap_in:
        c.wait_recv()
    qlane = lax.broadcasted_iota(jnp.int32, (CHUNK, 128), 1)
    mask_rows = qmask[...].astype(F32)
    for pair in range(HEADS // 2):
        both = qr[:, pair * 128 : (pair + 1) * 128].astype(F32)
        qrot[2 * pair] = jnp.where(qlane < ROPE, both, mask_rows).astype(BF16)
        qrot[2 * pair + 1] = jnp.where(qlane < ROPE, pltpu.roll(both, ROPE, 1), mask_rows).astype(BF16)

    for d in (2, 6, 1, 7, 4, 3, 5):
        spread(d).wait_recv()
        forward_unit(d).start()

    def block_ref(px, pzl, pc, start=0, size=ROWS):
        return lat.at[at_rows(seq_at(px, pzl, pc) * ROWS + start, size, 128)]

    own_block = block_ref(x, zl, core)

    def send_x(i):
        return remote(own_block, own_block, x_send.at[i], x_recv.at[i], chip_x((1, 3, 2)[i]))

    def recv_x(i):
        ref = block_ref((x + (3, 1, 2)[i]) % 4, zl, core)
        return remote(ref, ref, x_send.at[i], x_recv.at[i], sibling)

    z_dx = (0, 1, 3, 2)

    def send_z(j, half):
        ref = block_ref((x + z_dx[j]) % 4, zl, core, half * 128, 128)
        return remote(ref, ref, z_send.at[j, half], z_recv.at[j, half], chip_z((1, 3)[half]))

    def recv_z(j, half):
        ref = block_ref((x + z_dx[j]) % 4, 1 - zl, core, half * 128, 128)
        return remote(ref, ref, z_send.at[j, half], z_recv.at[j, half], sibling)

    order = ((0, 0), (0, 1), (1, 0), (3, 0), (2, 0), (1, 1), (3, 1), (2, 1))

    def pass_on(i):
        dx, dz = order[i]
        ref = block_ref((x + dx) % 4, (zl + dz) % 2, core)
        return remote(ref, ref, d_send.at[i], d_recv.at[i], sibling)

    def pass_in(i):
        dx, dz = order[i]
        ref = block_ref((x + dx) % 4, (zl + dz) % 2, other)
        return remote(ref, ref, d_send.at[i], d_recv.at[i], sibling)

    send_z(0, 0).start()
    send_z(0, 1).start()
    send_x(0).start()
    send_x(1).start()
    for d in range(8):
        forward_in(d).wait_recv()

    def work(index, first):
        rows = at_rows(index * CHUNK, CHUNK, CHUNK)
        made = {}

        def scores(h):
            pair, side = h // 2, h % 2
            if pair not in made:
                cols = slice(pair * 256, (pair + 1) * 256)
                keys = jnp.dot(lat[rows, :LATENT], wk[:, cols], preferred_element_type=F32).astype(BF16)
                vals = lax.dot_general(
                    wvt[cols, :], lat[rows, :LATENT], NT, preferred_element_type=F32
                ).astype(BF16)
                made[pair] = (keys, vals)
            keys = made[pair][0][:, side * 128 : (side + 1) * 128]
            left = jnp.concatenate([keys, lat[rows, LATENT:]], 1)
            right = jnp.concatenate([qn[:, h * 128 : (h + 1) * 128], qrot[h]], 1)
            s = lax.dot_general(left, right, NT, preferred_element_type=F32)
            if first:
                t = tri[...]
                parts = []
                for b in range(4):
                    row = s[b * 128 : (b + 1) * 128]
                    pieces = [row[:, c * 128 : (c + 1) * 128] for c in range(4)]
                    pieces[b] = pieces[b] + t
                    parts.append(jnp.concatenate(pieces, 1))
                s = jnp.concatenate(parts, 0)
            return s

        def finish(h, s):
            s3 = s.reshape(CHUNK // 8, 8, CHUNK)
            if first:
                m = jnp.max(jnp.max(s3, 0), 0, keepdims=True) * SCALE2 + SLACK
                m = jnp.broadcast_to(m, (8, CHUNK))
                shift[h] = m
            else:
                m = shift[h]
            w = jnp.exp2(s3 * SCALE2 - m[None])
            total[h] = total[h] + jnp.sum(w, 0)
            vals = made[h // 2][1][(h % 2) * 128 : (h % 2 + 1) * 128]
            acc[h] = acc[h] + jnp.dot(vals, w.reshape(CHUNK, CHUNK).astype(BF16), preferred_element_type=F32)

        held = scores(0)
        for h in range(HEADS):
            nxt = scores(h + 1) if h + 1 < HEADS else None
            finish(h, held)
            held = nxt

    def keep(index, step):
        rows = at_rows(index * CHUNK, CHUNK, CHUNK)
        return pltpu.make_async_copy(lat.at[rows], all_hbm.at[rows], all_sem.at[step])

    keep(seq // 2, 0).start()
    work(seq // 2, True)

    def step_body(step, carry):
        @pl.when(step == 1)
        def _():
            recv_z(0, 0).wait_recv()
            recv_z(0, 1).wait_recv()
            pass_on(1).start()
            send_x(2).start()
            pass_in(1).wait_recv()

        @pl.when(step == 2)
        def _():
            recv_x(1).wait_recv()
            pass_on(2).start()
            send_z(1, 0).start()
            send_z(1, 1).start()
            recv_x(0).wait_recv()
            pass_on(3).start()
            send_z(2, 0).start()
            send_z(2, 1).start()
            pass_in(2).wait_recv()

        @pl.when(step == 3)
        def _():
            pass_in(3).wait_recv()

        @pl.when(step == 4)
        def _():
            recv_x(2).wait_recv()
            pass_on(4).start()
            send_z(3, 0).start()
            send_z(3, 1).start()
            recv_z(1, 0).wait_recv()
            recv_z(1, 1).wait_recv()
            pass_on(5).start()
            pass_in(4).wait_recv()

        @pl.when(step == 5)
        def _():
            recv_z(2, 0).wait_recv()
            recv_z(2, 1).wait_recv()
            pass_on(6).start()
            pass_in(5).wait_recv()

        @pl.when(step == 6)
        def _():
            recv_z(3, 0).wait_recv()
            recv_z(3, 1).wait_recv()
            pass_on(7).start()
            pass_in(6).wait_recv()

        @pl.when(step == 7)
        def _():
            pass_in(7).wait_recv()

        far = jnp.where(step >= 5, step - 3, step)
        dx = jnp.where(far == 2, 1, jnp.where(far == 3, 3, jnp.where(far == 4, 2, 0)))
        dz = jnp.where(step >= 5, 1, jnp.where(step == 1, 1, 0))
        index = ((x + dx) % 4) * 2 + (zl + dz) % 2
        keep(index, step).start()
        work(index, False)
        return carry

    lax.fori_loop(1, 8, step_body, 0)

    def give(h):
        cols = at_rows(core * COLS + h * 128, 128, 128)
        here = slice(h * 128, (h + 1) * 128)
        return (
            pltpu.make_async_copy(done.at[mine, here], out_hbm.at[:, cols], o_loc.at[h]),
            remote(done.at[theirs, here], out_hbm.at[:, cols], o_send.at[h], o_recv.at[h], sibling),
        )

    most = None
    for h in range(HEADS):
        row = jnp.sum(total[h], 0, keepdims=True)
        most = row if most is None else jnp.maximum(most, row)
        done[:, h * 128 : (h + 1) * 128] = (acc[h] / row).T.astype(BF16)
        for c in give(h):
            c.start()
    peak[0] = jnp.broadcast_to(most[:, :ROWS], (8, ROWS))
    peak[1] = jnp.broadcast_to(most[:, ROWS:], (8, ROWS))
    tell = remote(peak.at[other], peak_ref.at[core], o_send.at[HEADS], o_recv.at[HEADS], sibling)
    tell.start()
    peak_ref[core] = peak[core]

    for c in swap:
        c.wait_send()
    for d in range(1, 8):
        spread(d).wait_send()
    for d in range(8):
        forward_unit(d).wait_send()
    for i in range(3):
        send_x(i).wait_send()
    for j in range(4):
        for half in range(2):
            send_z(j, half).wait_send()
    for i in range(1, 8):
        pass_on(i).wait_send()
    for i in range(8):
        keep(0, i).wait()
    for h in range(HEADS):
        here, there = give(h)
        here.wait()
        there.wait_send()
        cols = at_rows(other * COLS + h * 128, 128, 128)
        into = out_hbm.at[:, cols]
        remote(into, into, o_send.at[h], o_recv.at[h], sibling).wait_recv()
    tell.wait_send()
    into = peak_ref.at[other]
    remote(into, into, o_send.at[HEADS], o_recv.at[HEADS], sibling).wait_recv()


def settle(
    peak_ref, pos_ref, fast_hbm, all_hbm, qn_hbm, qr_hbm, wk_hbm, wv_hbm, out_hbm,
    lat, wk, wv, qn, qr, acc, total, top, result, sem,
):
    whole = pltpu.make_async_copy(fast_hbm, out_hbm, sem)
    whole.start()
    whole.wait()
    bad = jnp.logical_not(jnp.max(peak_ref[...]) <= 1.0)

    @pl.when(bad)
    def _():
        seq = lax.axis_index("seq")
        core = seq % 2

        def fetch(src, dst):
            c = pltpu.make_async_copy(src, dst, sem)
            c.start()
            c.wait()

        fetch(all_hbm, lat)
        qmask = query_mask(pos_ref).astype(F32)
        qlane = lax.broadcasted_iota(jnp.int32, (ROWS, 128), 1)

        def one_pair(pair, carry):
            pair_cols = at_rows(pair * 256, 256, 256)
            fetch(wk_hbm.at[:, pair_cols], wk)
            fetch(wv_hbm.at[:, pair_cols], wv)
            fetch(qn_hbm.at[:, pair_cols], qn)
            fetch(qr_hbm.at[:, at_rows(pair * 128, 128, 128)], qr)
            for side in range(2):
                cols = slice(side * 128, (side + 1) * 128)
                both = qr[...].astype(F32)
                if side:
                    both = pltpu.roll(both, ROPE, 1)
                rot = jnp.where(qlane < ROPE, both, qmask).astype(BF16)
                right = jnp.concatenate([qn[:, cols], rot], 1)
                acc[...] = jnp.zeros_like(acc)
                total[...] = jnp.zeros_like(total)
                top[...] = jnp.full_like(top, MASKED)

                def one_block(i, c):
                    index = (seq + i) % 16
                    rows = at_rows(index * ROWS, ROWS, ROWS)
                    here = lat[rows, :LATENT]
                    keys = jnp.dot(here, wk[:, cols], preferred_element_type=F32).astype(BF16)
                    vals = jnp.dot(here, wv[:, cols], preferred_element_type=F32).astype(BF16)
                    left = jnp.concatenate([keys, lat[rows, LATENT:]], 1)
                    s = lax.dot_general(right, left, NT, preferred_element_type=F32)
                    q = lax.broadcasted_iota(jnp.int32, (ROWS, ROWS), 0)
                    k = lax.broadcasted_iota(jnp.int32, (ROWS, ROWS), 1)
                    hidden = (i == 0) & (q // 128 == k // 128) & (k > q)
                    s = jnp.where(hidden, MASKED, s) * SCALE2
                    new = jnp.maximum(top[...], jnp.max(s, 1, keepdims=True))
                    w = jnp.exp2(s - new[:, :1])
                    factor = jnp.exp2(top[...] - new)
                    total[...] = total[...] * factor + jnp.sum(w, 1, keepdims=True)
                    acc[...] = acc[...] * factor + jnp.dot(w.astype(BF16), vals, preferred_element_type=F32)
                    top[...] = new
                    return c

                lax.fori_loop(0, 16, one_block, 0)
                result[:, cols] = (acc[...] / total[...]).astype(BF16)
            fetch(result, out_hbm.at[:, pair_cols])
            return carry

        lax.fori_loop(0, 8, one_pair, 0)


def per_device(q_nope, q_rope, latent, k_rope, positions, w_uk, w_uv):
    any_spec = pl.BlockSpec(memory_space=pl.ANY)
    vmem = pl.BlockSpec(memory_space=pltpu.VMEM)
    smem = pl.BlockSpec(memory_space=pltpu.SMEM)
    tokens = ROWS * 16
    dma = pltpu.SemaphoreType.DMA
    fast, rows, peak = pl.pallas_call(
        gather_attend,
        out_shape=(
            jax.ShapeDtypeStruct((ROWS, 2 * COLS), BF16),
            jax.ShapeDtypeStruct((tokens, WIDE), BF16),
            jax.ShapeDtypeStruct((2, 8, ROWS), F32),
        ),
        in_specs=[smem, vmem, vmem] + [any_spec] * 4,
        out_specs=(any_spec, any_spec, vmem),
        scratch_shapes=[
            pltpu.VMEM((UNIT, WIDE), BF16),
            pltpu.VMEM((tokens, WIDE), BF16),
            pltpu.VMEM((LATENT, COLS), BF16),
            pltpu.VMEM((LATENT, COLS), BF16),
            pltpu.VMEM((COLS, LATENT), BF16),
            pltpu.VMEM((CHUNK, COLS), BF16),
            pltpu.VMEM((CHUNK, COLS // 2), BF16),
            pltpu.VMEM((CHUNK, 128), BF16),
            pltpu.VMEM((HEADS, CHUNK, 128), BF16),
            pltpu.VMEM((128, 128), F32),
            pltpu.VMEM((HEADS, 128, CHUNK), F32),
            pltpu.VMEM((HEADS, 8, CHUNK), F32),
            pltpu.VMEM((HEADS, 8, CHUNK), F32),
            pltpu.VMEM((CHUNK, COLS), BF16),
            pltpu.VMEM((2, 8, ROWS), F32),
            dma((4,)),
            dma((3,)), dma((3,)),
            dma((8,)), dma((8,)),
            dma((8,)), dma((8,)),
            dma((3,)), dma((3,)),
            dma((4, 2)), dma((4, 2)),
            dma((8,)), dma((8,)),
            dma((HEADS,)),
            dma((HEADS + 1,)), dma((HEADS + 1,)),
            dma((8,)),
        ],
        compiler_params=pltpu.CompilerParams(
            collective_id=0, has_side_effects=True, vmem_limit_bytes=56 * 2**20
        ),
        cost_estimate=pl.CostEstimate(flops=26 * 10**9, bytes_accessed=12 * 2**20, transcendentals=17 * 10**6),
        name="gather_attend",
    )(positions, latent, k_rope, q_nope, q_rope, w_uk, w_uv)
    return pl.pallas_call(
        settle,
        out_shape=jax.ShapeDtypeStruct((ROWS, 2 * COLS), BF16),
        in_specs=[vmem, smem] + [any_spec] * 6,
        out_specs=any_spec,
        scratch_shapes=[
            pltpu.VMEM((tokens, WIDE), BF16),
            pltpu.VMEM((LATENT, 256), BF16),
            pltpu.VMEM((LATENT, 256), BF16),
            pltpu.VMEM((ROWS, 256), BF16),
            pltpu.VMEM((ROWS, 128), BF16),
            pltpu.VMEM((ROWS, 128), F32),
            pltpu.VMEM((ROWS, 128), F32),
            pltpu.VMEM((ROWS, 128), F32),
            pltpu.VMEM((ROWS, 256), BF16),
            pltpu.SemaphoreType.DMA,
        ],
        compiler_params=pltpu.CompilerParams(vmem_limit_bytes=32 * 2**20),
        name="settle",
    )(peak, positions, fast, rows, q_nope, q_rope, w_uk, w_uv)


def solution(mesh):
    in_specs = (
        P("seq", "head"),
        P("seq", "head"),
        P(("seq", "head"), None),
        P(("seq", "head"), None),
        P("seq"),
        P(None, "head"),
        P(None, "head"),
    )
    return jax.shard_map(
        per_device, mesh=mesh, in_specs=in_specs, out_specs=P("seq", "head"), check_vma=False
    )
```

time: 411 us -> 58.5 us (0.14); the launches traced: 405 us -> 58.3 us
  starting transfers between devices: 127 us -> 0 us
  matrix products: 111 us -> 0 us
  blocking collectives: 60.8 us -> 0 us
  Pallas kernels: 0 us -> 53.8 us
  other arithmetic: 46.9 us -> 0 us
  local copies, waits for them, and re-layouts: 25.2 us -> 4.44 us
  loops' own time: 19.9 us -> 0 us
  waiting for transfers between devices: 13.2 us -> 0 us
    ppermute x45 -> x0, starting transfers between devices: 127 us -> none  [from_behind(): return lax.ppermute(block, axis, route)]
    dot_general x70 -> x0, matrix products: 111 us -> none  [the longest x14 32.4 us: compute(): jnp.dot(lat_rows, w_uk, preferred_element_type=jnp.float32)]
    all_gather x2 -> x0, blocking collectives: 60.8 us -> none  [the longest x1 32.3 us: per_device(): lax.all_gather(latent, 'head', axis=0, tiled=True)]
    pallas_call x0 -> x2, Pallas kernels: none -> 53.8 us  [the longest x1 52.1 us: per_device(): pl.pallas_call(gather_attend, out_shape=(jax.ShapeDtypeStruct((ROWS, 2 *...]
    another operation x17 -> x0, loops' own time: 19.9 us -> none  [the longest x1 18.7 us: per_device(): lax.fori_loop(0, cycle_len - 1, cycle_turn, (state, own_block))]
    ppermute x45 -> x0, waiting for transfers between devices: 13.2 us -> none  [from_behind(): return lax.ppermute(block, axis, route)]
    while x47 -> x0, local copies, waits for them, and re-layouts: 12.4 us -> none
    max x13 -> x0, other arithmetic: 11.3 us -> none  [compute(): new_top = jnp.maximum(top, jnp.max(scores, axis=2))]
  transfers between devices with their start and end apart: 45 -> 0, of which waited for: 15 -> 0; matrix products, arithmetic and copies ran while one was open for 2% -> 0% of each run, Pallas kernels for 0% -> 0%
where the time goes in v1:
time: 58.5 us; the launch traced here: 58.3 us
  Pallas kernels  53.8 us (92%)
  local copies, waits for them, and re-layouts  4.44 us (8%)
    pallas_call x1, Pallas kernels, per_device(): pl.pallas_call(gather_attend, out_shape=(jax.ShapeDtypeStruct((ROWS, 2 *...  52.1 us
    unnamed x16, local copies, waits for them, and re-layouts  4.44 us
    pallas_call x1, Pallas kernels, per_device(): pl.pallas_call(settle, out_shape=jax.ShapeDtypeStruct((ROWS, 2 * COLS), B...  1.65 us

profile of v1, /device:TPU:1, one launch (start us, length us, event | category | flops | bytes accessed | tf_op | source)
XLA Modules:
  0.0 58.3 jit_solution(13330540652477429181)
XLA Ops:
  0.0 0.0 copy-start.2
  0.0 0.0 copy-start.1
  0.0 0.0 copy-start.7
  0.0 0.0 copy-start.5
  0.0 0.0 copy-start.3
  0.0 52.1 %gather_attend.1 = (bf16[256,2048]{1,0:T(8,128)(2,1)}, bf16[4096,640]{1,0:T(8,128)(2,1)}, f32[2,8,256]{2,1,0:T(8,128)}) custom-call(s32[256]{0:T(256)} %pos_ref.3, bf16[32,512]{1,0:T(8,128)(2,1)} %lat_ref.1, bf16[32,64]{1,0:T(8,128)(2,1)} %rot_ref.1, bf16[256,2048]{1,0:T(8,128)(2,1)} %qn_hbm.3, bf16[256,1024]{1,0:T(8,128)(2,1)} %qr_hbm.3, ...), custom_call_target="tpu_custom_call" | custom-call | flops 25999998976 | bytes 12582912 | tf_op jit(solution)/shard_map/gather_attend/pallas_call | solution.py:449
  52.2 0.0 copy-done.2
  52.2 0.0 copy-done.1
  52.2 0.0 copy-done.7
  52.2 0.0 copy-done.5
  52.2 0.0 copy-done.3
  52.2 0.0 copy-start
  52.2 2.5 %copy-done = bf16[4096,640]{1,0:T(8,128)(2,1)S(1)} copy-done((bf16[4096,640]{1,0:T(8,128)(2,1)S(1)}, bf16[4096,640]{1,0:T(8,128)(2,1)}, u32[]{:S(2)}) %copy-start) | copy-done | bytes 5242904
  54.7 0.0 copy-start.4
  54.7 1.2 %copy-done.4 = bf16[256,2048]{1,0:T(8,128)(2,1)S(1)} copy-done((bf16[256,2048]{1,0:T(8,128)(2,1)S(1)}, bf16[256,2048]{1,0:T(8,128)(2,1)}, u32[]{:S(2)}) %copy-start.4) | copy-done | bytes 1048600
  55.9 0.0 copy-start.6
  55.9 0.7 %copy-done.6 = f32[2,8,256]{2,1,0:T(8,128)S(1)} copy-done((f32[2,8,256]{2,1,0:T(8,128)S(1)}, f32[2,8,256]{2,1,0:T(8,128)}, u32[]{:S(2)}) %copy-start.6) | copy-done | bytes 16408
  56.7 1.6 %settle.1 = bf16[256,2048]{1,0:T(8,128)(2,1)} custom-call(f32[2,8,256]{2,1,0:T(8,128)S(1)} %copy-done.6, s32[256]{0:T(256)S(1)} %copy-done.7, bf16[256,2048]{1,0:T(8,128)(2,1)S(1)} %copy-done.4, bf16[4096,640]{1,0:T(8,128)(2,1)S(1)} %copy-done, bf16[256,2048]{1,0:T(8,128)(2,1)S(1)} %copy-done.3, bf16[256,1024]{1,0:T(8,128)(2,1)S(1)} %copy-done.5, ...), custom_call_target="tpu_custom_call" | custom-call | tf_op jit(solution)/shard_map/settle/pallas_call | solution.py:491
Async XLA Ops:
  0.0 52.2 %copy-start.2 = (bf16[512,2048]{1,0:T(8,128)(2,1)S(1)}, bf16[512,2048]{1,0:T(8,128)(2,1)}, u32[]{:S(2)}) copy-start(bf16[512,2048]{1,0:T(8,128)(2,1)} %wv_hbm.3) | copy-start | bytes 6291460
  0.0 52.2 %copy-start.1 = (bf16[512,2048]{1,0:T(8,128)(2,1)S(1)}, bf16[512,2048]{1,0:T(8,128)(2,1)}, u32[]{:S(2)}) copy-start(bf16[512,2048]{1,0:T(8,128)(2,1)} %wk_hbm.3) | copy-start | bytes 6291460
  0.0 52.2 %copy-start.7 = (s32[256]{0:T(256)S(1)}, s32[256]{0:T(256)}, u32[]{:S(2)}) copy-start(s32[256]{0:T(256)} %pos_ref.3) | copy-start | bytes 3076
  0.0 52.2 %copy-start.5 = (bf16[256,1024]{1,0:T(8,128)(2,1)S(1)}, bf16[256,1024]{1,0:T(8,128)(2,1)}, u32[]{:S(2)}) copy-start(bf16[256,1024]{1,0:T(8,128)(2,1)} %qr_hbm.3) | copy-start | bytes 1572868
  0.0 52.2 %copy-start.3 = (bf16[256,2048]{1,0:T(8,128)(2,1)S(1)}, bf16[256,2048]{1,0:T(8,128)(2,1)}, u32[]{:S(2)}) copy-start(bf16[256,2048]{1,0:T(8,128)(2,1)} %qn_hbm.3) | copy-start | bytes 3145732
  52.2 2.5 %copy-start = (bf16[4096,640]{1,0:T(8,128)(2,1)S(1)}, bf16[4096,640]{1,0:T(8,128)(2,1)}, u32[]{:S(2)}) copy-start(bf16[4096,640]{1,0:T(8,128)(2,1)} %get-tuple-element.10.all_hbm) | copy-start | bytes 15728644
  54.7 1.2 %copy-start.4 = (bf16[256,2048]{1,0:T(8,128)(2,1)S(1)}, bf16[256,2048]{1,0:T(8,128)(2,1)}, u32[]{:S(2)}) copy-start(bf16[256,2048]{1,0:T(8,128)(2,1)} %get-tuple-element.9.fast_hbm) | copy-start | bytes 3145732
  55.9 0.7 %copy-start.6 = (f32[2,8,256]{2,1,0:T(8,128)S(1)}, f32[2,8,256]{2,1,0:T(8,128)}, u32[]{:S(2)}) copy-start(f32[2,8,256]{2,1,0:T(8,128)} %get-tuple-element.8.peak_ref) | copy-start | bytes 49156

commit v2 on v1

--- a/solution.py
+++ b/solution.py
@@ -47,8 +47,8 @@
     pos_ref, lat_ref, rot_ref, qn_hbm, qr_hbm, wk_hbm, wv_hbm,
     out_hbm, all_hbm, peak_ref,
     unit, lat, wk, wv, wvt, qn, qr, qmask, qrot, tri, acc, total, shift, done, peak,
-    loc_sem, q_send, q_recv, h_send, h_recv, f_send, f_recv, x_send, x_recv, z_send, z_recv,
-    d_send, d_recv, o_loc, o_send, o_recv, all_sem,
+    loc_sem, q_send, q_recv, h_send, h_recv, f_send, f_recv, x_send, x_recv, far_send, far_recv,
+    u_send, u_recv, z_send, z_recv, d_send, d_recv, o_loc, o_send, o_recv, all_sem,
 ):
     seq = lax.axis_index("seq")
     head = lax.axis_index("head")
@@ -67,11 +67,12 @@
         pz = (z + d) % 4
         return (seq_at(x, pz % 2, core), y * 2 + pz // 2)
 
-    def chip_h(d):
-        return (seq, (head + d) % 8)
+    def chip_h(i):
+        dy, dzh = i // 2, i % 2
+        return (seq, ((y + dy) % 4) * 2 + (zh + dzh) % 2)
 
     sibling = (seq_at(x, zl, other), head)
-    partners = [chip_h(d) for d in range(1, 8)] + [chip_x(1), chip_x(3), chip_x(2), chip_z(1), chip_z(3), sibling]
+    partners = [chip_h(i) for i in range(1, 8)] + [chip_x(1), chip_x(3), chip_z(1), chip_z(3), sibling]
 
     barrier = pltpu.get_barrier_semaphore()
     for p in partners:
@@ -108,22 +109,46 @@
             src_ref=src, dst_ref=dst, send_sem=send, recv_sem=recv, device_id=to, device_id_type=MESH
         )
 
-    def unit_rows(d):
-        return lat.at[at_rows(seq * ROWS + ((head + 8 - d) % 8) * UNIT, UNIT, UNIT)]
-
-    def spread(d):
-        return remote(unit, lat.at[own_unit], h_send.at[d], h_recv.at[d], chip_h(d))
-
-    def forward_unit(d):
-        src = unit_rows(d)
-        return remote(src, src, f_send.at[d], f_recv.at[d], sibling)
-
-    def forward_in(d):
-        dst = lat.at[at_rows(seq_at(x, zl, other) * ROWS + ((head + 8 - d) % 8) * UNIT, UNIT, UNIT)]
-        return remote(dst, dst, f_send.at[d], f_recv.at[d], sibling)
-
-    for d in (4, 2, 6, 1, 7, 3, 5):
-        spread(d).start()
+    def unit_ref(sq, i, own_zh):
+        h = ((y + 4 - i // 2) % 4) * 2 + (own_zh + i) % 2
+        return lat.at[at_rows(sq * ROWS + h * UNIT, UNIT, UNIT)]
+
+    def spread(i):
+        return remote(unit, lat.at[own_unit], h_send.at[i], h_recv.at[i], chip_h(i))
+
+    def spread_in(i):
+        ref = unit_ref(seq, i, zh)
+        return remote(ref, ref, h_send.at[i], h_recv.at[i], sibling)
+
+    def forward_unit(i):
+        src = unit_ref(seq, i, zh)
+        return remote(src, src, f_send.at[i], f_recv.at[i], sibling)
+
+    def forward_in(i):
+        dst = unit_ref(seq_at(x, zl, other), i, zh)
+        return remote(dst, dst, f_send.at[i], f_recv.at[i], sibling)
+
+    def unit_x(i, way):
+        src = unit_ref(seq, i, zh)
+        return remote(src, src, x_send.at[way, i], x_recv.at[way, i], chip_x((1, 3)[way]))
+
+    def unit_x_in(i, way):
+        dst = unit_ref(seq_at((x + (3, 1)[way]) % 4, zl, core), i, zh)
+        return remote(dst, dst, x_send.at[way, i], x_recv.at[way, i], sibling)
+
+    def unit_z(i):
+        src = unit_ref(seq, i, zh)
+        return remote(src, src, u_send.at[i], u_recv.at[i], chip_z((1, 3)[(i // 2) % 2]))
+
+    def unit_z_in(i):
+        from_zh = ((z + (3, 1)[(i // 2) % 2]) % 4) // 2
+        dst = unit_ref(seq_at(x, 1 - zl, core), i, from_zh)
+        return remote(dst, dst, u_send.at[i], u_recv.at[i], sibling)
+
+    for i in (1, 5, 3, 7, 4, 2, 6):
+        spread(i).start()
+    unit_x(0, 0).start()
+    unit_x(0, 1).start()
     swap = [
         remote(qn_hbm.at[:, their_cols], qn.at[mine], q_send.at[0], q_recv.at[0], sibling),
         remote(
@@ -141,6 +166,7 @@
         remote(qmask.at[theirs], qmask.at[theirs], q_send.at[2], q_recv.at[2], sibling),
     ]
     forward_unit(0).start()
+    unit_z(0).start()
 
     key = lax.broadcasted_iota(jnp.int32, (128, 128), 0)
     query = lax.broadcasted_iota(jnp.int32, (128, 128), 1)
@@ -161,21 +187,23 @@
         qrot[2 * pair] = jnp.where(qlane < ROPE, both, mask_rows).astype(BF16)
         qrot[2 * pair + 1] = jnp.where(qlane < ROPE, pltpu.roll(both, ROPE, 1), mask_rows).astype(BF16)
 
-    for d in (2, 6, 1, 7, 4, 3, 5):
-        spread(d).wait_recv()
-        forward_unit(d).start()
+    for i in (2, 6, 4, 1, 3, 7, 5):
+        spread_in(i).wait_recv()
+        forward_unit(i).start()
+        unit_z(i).start()
+        unit_x(i, 0).start()
+        unit_x(i, 1).start()
 
     def block_ref(px, pzl, pc, start=0, size=ROWS):
         return lat.at[at_rows(seq_at(px, pzl, pc) * ROWS + start, size, 128)]
 
-    own_block = block_ref(x, zl, core)
-
-    def send_x(i):
-        return remote(own_block, own_block, x_send.at[i], x_recv.at[i], chip_x((1, 3, 2)[i]))
-
-    def recv_x(i):
-        ref = block_ref((x + (3, 1, 2)[i]) % 4, zl, core)
-        return remote(ref, ref, x_send.at[i], x_recv.at[i], sibling)
+    def send_far(half):
+        ref = block_ref((x + (3, 1)[half]) % 4, zl, core, half * 128, 128)
+        return remote(ref, ref, far_send.at[half], far_recv.at[half], chip_x((1, 3)[half]))
+
+    def recv_far(half):
+        ref = block_ref((x + 2) % 4, zl, core, half * 128, 128)
+        return remote(ref, ref, far_send.at[half], far_recv.at[half], sibling)
 
     z_dx = (0, 1, 3, 2)
 
@@ -199,12 +227,8 @@
         ref = block_ref((x + dx) % 4, (zl + dz) % 2, other)
         return remote(ref, ref, d_send.at[i], d_recv.at[i], sibling)
 
-    send_z(0, 0).start()
-    send_z(0, 1).start()
-    send_x(0).start()
-    send_x(1).start()
-    for d in range(8):
-        forward_in(d).wait_recv()
+    for i in range(8):
+        forward_in(i).wait_recv()
 
     def work(index, first):
         rows = at_rows(index * CHUNK, CHUNK, CHUNK)
@@ -263,34 +287,33 @@
     def step_body(step, carry):
         @pl.when(step == 1)
         def _():
-            recv_z(0, 0).wait_recv()
-            recv_z(0, 1).wait_recv()
+            for i in range(8):
+                unit_z_in(i).wait_recv()
             pass_on(1).start()
-            send_x(2).start()
+            for way in (1, 0):
+                for i in range(8):
+                    unit_x_in(i, way).wait_recv()
+                send_far(way).start()
+                pass_on((3, 2)[way]).start()
+                send_z((2, 1)[way], 0).start()
+                send_z((2, 1)[way], 1).start()
             pass_in(1).wait_recv()
 
         @pl.when(step == 2)
         def _():
-            recv_x(1).wait_recv()
-            pass_on(2).start()
-            send_z(1, 0).start()
-            send_z(1, 1).start()
-            recv_x(0).wait_recv()
-            pass_on(3).start()
-            send_z(2, 0).start()
-            send_z(2, 1).start()
             pass_in(2).wait_recv()
 
         @pl.when(step == 3)
         def _():
-            pass_in(3).wait_recv()
-
-        @pl.when(step == 4)
-        def _():
-            recv_x(2).wait_recv()
+            recv_far(0).wait_recv()
+            recv_far(1).wait_recv()
             pass_on(4).start()
             send_z(3, 0).start()
             send_z(3, 1).start()
+            pass_in(3).wait_recv()
+
+        @pl.when(step == 4)
+        def _():
             recv_z(1, 0).wait_recv()
             recv_z(1, 1).wait_recv()
             pass_on(5).start()
@@ -347,14 +370,16 @@
 
     for c in swap:
         c.wait_send()
-    for d in range(1, 8):
-        spread(d).wait_send()
-    for d in range(8):
-        forward_unit(d).wait_send()
-    for i in range(3):
-        send_x(i).wait_send()
-    for j in range(4):
-        for half in range(2):
+    for i in range(8):
+        if i:
+            spread(i).wait_send()
+        forward_unit(i).wait_send()
+        unit_z(i).wait_send()
+        unit_x(i, 0).wait_send()
+        unit_x(i, 1).wait_send()
+    for half in range(2):
+        send_far(half).wait_send()
+        for j in range(1, 4):
             send_z(j, half).wait_send()
     for i in range(1, 8):
         pass_on(i).wait_send()
@@ -373,13 +398,16 @@
 
 
 def settle(
-    peak_ref, pos_ref, fast_hbm, all_hbm, qn_hbm, qr_hbm, wk_hbm, wv_hbm, out_hbm,
-    lat, wk, wv, qn, qr, acc, total, top, result, sem,
+    peak_hbm, pos_ref, fast_hbm, all_hbm, qn_hbm, qr_hbm, wk_hbm, wv_hbm, out_hbm,
+    peak, lat, wk, wv, qn, qr, acc, total, top, result, sem, peak_sem,
 ):
     whole = pltpu.make_async_copy(fast_hbm, out_hbm, sem)
     whole.start()
+    look = pltpu.make_async_copy(peak_hbm, peak, peak_sem)
+    look.start()
+    look.wait()
+    bad = jnp.logical_not(jnp.max(peak[...]) <= 1.0)
     whole.wait()
-    bad = jnp.logical_not(jnp.max(peak_ref[...]) <= 1.0)
 
     @pl.when(bad)
     def _():
@@ -441,7 +469,7 @@
 
 
 def per_device(q_nope, q_rope, latent, k_rope, positions, w_uk, w_uv):
-    any_spec = pl.BlockSpec(memory_space=pl.ANY)
+    hbm = pl.BlockSpec(memory_space=pltpu.HBM)
     vmem = pl.BlockSpec(memory_space=pltpu.VMEM)
     smem = pl.BlockSpec(memory_space=pltpu.SMEM)
     tokens = ROWS * 16
@@ -453,8 +481,8 @@
             jax.ShapeDtypeStruct((tokens, WIDE), BF16),
             jax.ShapeDtypeStruct((2, 8, ROWS), F32),
         ),
-        in_specs=[smem, vmem, vmem] + [any_spec] * 4,
-        out_specs=(any_spec, any_spec, vmem),
+        in_specs=[smem, vmem, vmem] + [hbm] * 4,
+        out_specs=(hbm, hbm, vmem),
         scratch_shapes=[
             pltpu.VMEM((UNIT, WIDE), BF16),
             pltpu.VMEM((tokens, WIDE), BF16),
@@ -475,7 +503,9 @@
             dma((3,)), dma((3,)),
             dma((8,)), dma((8,)),
             dma((8,)), dma((8,)),
-            dma((3,)), dma((3,)),
+            dma((2, 8)), dma((2, 8)),
+            dma((2,)), dma((2,)),
+            dma((8,)), dma((8,)),
             dma((4, 2)), dma((4, 2)),
             dma((8,)), dma((8,)),
             dma((HEADS,)),
@@ -491,9 +521,10 @@
     return pl.pallas_call(
         settle,
         out_shape=jax.ShapeDtypeStruct((ROWS, 2 * COLS), BF16),
-        in_specs=[vmem, smem] + [any_spec] * 6,
-        out_specs=any_spec,
+        in_specs=[hbm, smem] + [hbm] * 6,
+        out_specs=hbm,
         scratch_shapes=[
+            pltpu.VMEM((2, 8, ROWS), F32),
             pltpu.VMEM((tokens, WIDE), BF16),
             pltpu.VMEM((LATENT, 256), BF16),
             pltpu.VMEM((LATENT, 256), BF16),
@@ -504,8 +535,9 @@
             pltpu.VMEM((ROWS, 128), F32),
             pltpu.VMEM((ROWS, 256), BF16),
             pltpu.SemaphoreType.DMA,
+            pltpu.SemaphoreType.DMA,
         ],
-        compiler_params=pltpu.CompilerParams(vmem_limit_bytes=32 * 2**20),
+        compiler_params=pltpu.CompilerParams(vmem_limit_bytes=64 * 2**20 - 2**16),
         name="settle",
     )(peak, positions, fast, rows, q_nope, q_rope, w_uk, w_uv)
 

time: 58.5 us -> 83.3 us (1.42)
  Pallas kernels: 53.8 us -> 83.1 us
  local copies, waits for them, and re-layouts: 4.44 us -> 0 us
    pallas_call x1, Pallas kernels: 1.65 us -> 33.6 us  [per_device(): pl.pallas_call(settle, out_shape=jax.ShapeDtypeStruct((ROWS, 2 * COLS), B...]
    unnamed x16 -> x0, local copies, waits for them, and re-layouts: 4.44 us -> none
    pallas_call x1, Pallas kernels: 52.1 us -> 49.5 us  [per_device(): pl.pallas_call(gather_attend, out_shape=(jax.ShapeDtypeStruct((ROWS, 2 *...]
where the time goes in v2:
time: 83.3 us; the launch traced here: 83.1 us
  Pallas kernels  83.1 us (100%)
    pallas_call x1, Pallas kernels, per_device(): pl.pallas_call(gather_attend, out_shape=(jax.ShapeDtypeStruct((ROWS, 2 *...  49.5 us
    pallas_call x1, Pallas kernels, per_device(): pl.pallas_call(settle, out_shape=jax.ShapeDtypeStruct((ROWS, 2 * COLS), B...  33.6 us

profile of v2, /device:TPU:1, one launch (start us, length us, event | category | flops | bytes accessed | tf_op | source)
XLA Modules:
  0.0 83.1 jit_solution(11243740915560449502)
XLA Ops:
  0.0 49.5 %gather_attend.1 = (bf16[256,2048]{1,0:T(8,128)(2,1)}, bf16[4096,640]{1,0:T(8,128)(2,1)}, f32[2,8,256]{2,1,0:T(8,128)}) custom-call(s32[256]{0:T(256)} %pos_ref.3, bf16[32,512]{1,0:T(8,128)(2,1)} %lat_ref.1, bf16[32,64]{1,0:T(8,128)(2,1)} %rot_ref.1, bf16[256,2048]{1,0:T(8,128)(2,1)} %qn_hbm.3, bf16[256,1024]{1,0:T(8,128)(2,1)} %qr_hbm.3, ...), custom_call_target="tpu_custom_call" | custom-call | flops 25999998976 | bytes 12582912 | tf_op jit(solution)/shard_map/gather_attend/pallas_call | solution.py:477
  49.5 33.6 %settle.1 = bf16[256,2048]{1,0:T(8,128)(2,1)} custom-call(f32[2,8,256]{2,1,0:T(8,128)} %get-tuple-element.8.peak_hbm, s32[256]{0:T(256)} %pos_ref.3, bf16[256,2048]{1,0:T(8,128)(2,1)} %get-tuple-element.9.fast_hbm, bf16[4096,640]{1,0:T(8,128)(2,1)} %get-tuple-element.10.all_hbm, bf16[256,2048]{1,0:T(8,128)(2,1)} %qn_hbm.3, bf16[256,1024]{1,0:T(8,128)(2,1)} %qr_hbm.3, ...), custom_call_target="tpu_custom_call" | custom-call | tf_op jit(solution)/shard_map/settle/pallas_call | solution.py:521

commit v3 on v2

v3 whole, which is shorter than its diff:
```python
import functools
import math

import jax
import jax.numpy as jnp
from jax import lax
from jax.experimental import pallas as pl
from jax.experimental.pallas import tpu as pltpu
from jax.sharding import PartitionSpec as P

MESH = pl.DeviceIdType.MESH
F32 = jnp.float32
BF16 = jnp.bfloat16
NT = (((1,), (1,)), ((), ()))
NOPE = 128
ROPE = 64
LATENT = 512
WIDE = 640
ROWS = 256
CHUNK = 512
UNIT = 32
HEADS = 8
AHEAD = 3
COLS = HEADS * NOPE
SCALE2 = (NOPE + ROPE) ** (-0.5) * math.log2(math.e)
MASKED = -1e30
SHIFT = 576.0
LEAST = 2.0**-90


def both_signs(pattern):
    found = [()]
    for p in pattern:
        found = [f + (v,) for f in found for v in ((1, 3) if p == 1 else (p,))]
    return found


SLOTS = (
    [(0, 0, 0), (0, 1, 0), (0, 3, 0), (1, 0, 0), (3, 0, 0), (0, 0, 1), (0, 0, 3), (2, 0, 0)]
    + both_signs((1, 1, 0)) + both_signs((1, 0, 1))
    + both_signs((0, 1, 1)) + both_signs((2, 1, 0)) + both_signs((2, 0, 1))
    + both_signs((1, 2, 0)) + both_signs((0, 2, 1)) + both_signs((1, 0, 2)) + [(2, 2, 0), (2, 0, 2)]
    + both_signs((1, 1, 1))
    + both_signs((2, 1, 1)) + both_signs((1, 2, 1))
    + both_signs((1, 1, 2)) + both_signs((2, 2, 1)) + both_signs((1, 2, 2))
    + [(0, 2, 0), (0, 0, 2), (0, 1, 2), (0, 3, 2), (0, 2, 2), (2, 1, 2), (2, 3, 2), (2, 2, 2)]
)
Y2, Z2 = 56, 57
OWN_FIRST, OWN_LAST = 3, 5
STAGES = (
    list(range(1, 8)) + [Y2, Z2],
    list(range(8, 24)),
    list(range(24, 32)) + [58, 59, 60],
    list(range(32, 44)),
    list(range(44, 56)) + [61, 62, 63],
)


def plan_routes():
    place = {s: i for i, s in enumerate(SLOTS)}
    routes = {i: (SLOTS[i], 0) for i in STAGES[0]}
    first = {0} | set(STAGES[0])
    ready = (first, first, first, first | set(STAGES[1]), first | set(STAGES[1]) | set(range(24, 32)))
    for stages, have in (
        (STAGES[1] + STAGES[2], first),
        (STAGES[3], first | set(STAGES[1])),
        (STAGES[4], first | set(STAGES[1]) | set(range(24, 32))),
    ):
        load = {}
        options, taken = {}, {}
        for i in stages:
            options[i] = []
            for axis in range(3):
                for way in {0: (), 1: (1,), 3: (3,), 2: (1, 3, 2)}[SLOTS[i][axis]]:
                    step = tuple(way if a == axis else 0 for a in range(3))
                    parent = place[tuple((v - w) % 4 for v, w in zip(SLOTS[i], step))]
                    if parent in have:
                        links = [(axis, w) for w in ((1, 3) if way == 2 else (way,))]
                        options[i].append((step, parent, links))
            single = [o for o in options[i] if len(o[2]) == 1]
            options[i] = single or options[i]
        for i in stages * 6:
            for k in taken.get(i, ((), 0, ()))[2]:
                load[k] -= 1
            taken[i] = min(options[i], key=lambda o: (sum(load.get(k, 0) for k in o[2]) / len(o[2]), o[0], o[1]))
            for k in taken[i][2]:
                load[k] = load.get(k, 0) + 1
        for i in stages:
            routes[i] = taken[i][:2]
    return routes


ROUTES = plan_routes()


def at_rows(start, size, step):
    return pl.ds(pl.multiple_of(start, step), size)


def key_lanes(shape, block):
    return jnp.where(lax.broadcasted_iota(jnp.int32, shape, 1) - ROPE == block, 1.0, 0.0)


def query_mask(pos_ref):
    parts = []
    for i in range(2):
        lane = lax.broadcasted_iota(jnp.int32, (128, 128), 1) - ROPE
        value = jnp.where(lane > pos_ref[i * 128] // 128, MASKED, -SHIFT)
        parts.append(jnp.where((lane >= 0) & (lane < 32), value, 0.0))
    return jnp.concatenate(parts, 0).astype(BF16)


def head_of(slot, y, zh):
    _, dy, dz = SLOTS[slot]
    return ((y + dy) % 4) * 2 + (zh + dz // 2) % 2


def gather_attend(
    pos_ref, lat_ref, rot_ref, qn_hbm, qr_hbm, wk_hbm, wv_hbm,
    out_hbm, all_hbm, peak_ref,
    lat, wk, wv, wvt, qn, qr, qmask, qrot, hide, acc, total, done, peak,
    loc_sem, q_send, q_recv, u_send, u_recv, d_send, d_recv, o_loc, o_send, o_recv, all_sem,
):
    seq = lax.axis_index("seq")
    head = lax.axis_index("head")
    x, zl, core = seq // 4, (seq // 2) % 2, seq % 2
    y, zh = head // 2, head % 2
    z = zh * 2 + zl
    other = 1 - core

    def chip(back):
        px, py, pz = (x + 4 - back[0]) % 4, (y + 4 - back[1]) % 4, (z + 4 - back[2]) % 4
        return (px * 4 + (pz % 2) * 2 + core, py * 2 + pz // 2)

    sibling = (seq + 1 - 2 * core, head)
    partners = [chip(SLOTS[i]) for i in STAGES[0]] + [sibling]

    barrier = pltpu.get_barrier_semaphore()
    for p in partners:
        pl.semaphore_signal(barrier, inc=1, device_id=p, device_id_type=MESH)

    mine = at_rows(core * ROWS, ROWS, ROWS)
    theirs = at_rows(other * ROWS, ROWS, ROWS)
    mine_cols = at_rows(core * COLS, COLS, COLS)
    their_cols = at_rows(other * COLS, COLS, COLS)
    half_cols = COLS // 2
    local = [
        pltpu.make_async_copy(wv_hbm.at[:, mine_cols], wv, loc_sem.at[0]),
        pltpu.make_async_copy(wk_hbm.at[:, mine_cols], wk, loc_sem.at[1]),
        pltpu.make_async_copy(qn_hbm.at[:, mine_cols], qn.at[mine], loc_sem.at[2]),
        pltpu.make_async_copy(
            qr_hbm.at[:, at_rows(core * half_cols, half_cols, half_cols)], qr.at[mine], loc_sem.at[3]
        ),
    ]
    for c in local:
        c.start()

    block = jnp.where(head < 4, pos_ref[0] // 128, pos_ref[128] // 128)
    lane = lax.broadcasted_iota(jnp.int32, (UNIT, 128), 1)
    rot = jnp.concatenate([rot_ref[...].astype(F32), jnp.zeros((UNIT, ROPE), F32)], 1)
    lat[0, core, :, :LATENT] = lat_ref[...]
    lat[0, core, :, LATENT:] = jnp.where(lane < ROPE, rot, key_lanes((UNIT, 128), block)).astype(BF16)
    qmask[mine] = query_mask(pos_ref)

    pl.semaphore_wait(barrier, len(partners))

    def remote(src, dst, send, recv, to):
        return pltpu.make_async_remote_copy(
            src_ref=src, dst_ref=dst, send_sem=send, recv_sem=recv, device_id=to, device_id_type=MESH
        )

    def pass_unit(i):
        step, parent = ROUTES[i]
        return remote(lat.at[parent, core], lat.at[i, core], u_send.at[i], u_recv.at[i], chip(step))

    def unit_in(i):
        ref = lat.at[i, core]
        return remote(ref, ref, u_send.at[i], u_recv.at[i], sibling)

    def share(i, size, sem, side):
        ref = lat.at[pl.ds(i, size), side]
        return remote(ref, ref, d_send.at[sem], d_recv.at[sem], sibling)

    def share_chunk(k):
        return share(k * 8, 8, k, core)

    def chunk_in(k):
        return share(k * 8, 8, k, other)

    for i in STAGES[0]:
        pass_unit(i).start()
    swap = [
        remote(qn_hbm.at[:, their_cols], qn.at[mine], q_send.at[0], q_recv.at[0], sibling),
        remote(
            qr_hbm.at[:, at_rows(other * half_cols, half_cols, half_cols)], qr.at[mine],
            q_send.at[1], q_recv.at[1], sibling,
        ),
        remote(qmask.at[mine], qmask.at[mine], q_send.at[2], q_recv.at[2], sibling),
    ]
    for c in swap:
        c.start()
    swap_in = [
        remote(qn.at[theirs], qn.at[theirs], q_send.at[0], q_recv.at[0], sibling),
        remote(qr.at[theirs], qr.at[theirs], q_send.at[1], q_recv.at[1], sibling),
        remote(qmask.at[theirs], qmask.at[theirs], q_send.at[2], q_recv.at[2], sibling),
    ]

    qlane = lax.broadcasted_iota(jnp.int32, (ROWS, 128), 1)

    def prepare(rows):
        mask_rows = qmask[rows].astype(F32)
        for pair in range(HEADS // 2):
            both = qr[rows, pair * 128 : (pair + 1) * 128].astype(F32)
            qrot[2 * pair, rows] = jnp.where(qlane < ROPE, both, mask_rows).astype(BF16)
            qrot[2 * pair + 1, rows] = jnp.where(qlane < ROPE, pltpu.roll(both, ROPE, 1), mask_rows).astype(BF16)

    local[2].wait()
    local[3].wait()
    prepare(mine)
    key = lax.broadcasted_iota(jnp.int32, (UNIT, CHUNK), 0)
    query = lax.broadcasted_iota(jnp.int32, (UNIT, CHUNK), 1)
    for n, slot in enumerate(list(range(OWN_FIRST)) + list(range(56, 56 + OWN_LAST))):
        h = head_of(slot, y, zh)
        for side in range(2):
            hidden = (query // 128 == side * 2 + h // 4) & (key + side * ROWS + h * UNIT > query)
            hide[(n * 2 + side) * UNIT : (n * 2 + side + 1) * UNIT, :] = jnp.where(hidden, MASKED, 0.0)
    local[0].wait()
    for i in range(HEADS):
        wvt[i * 128 : (i + 1) * 128, :] = wv[:, i * 128 : (i + 1) * 128].T
    local[1].wait()

    for i in range(1, 4):
        unit_in(i).wait_recv()
    share(0, 4, 0, core).start()
    for i in range(4, 8):
        unit_in(i).wait_recv()
    share(4, 4, 8, core).start()
    for i in STAGES[1]:
        pass_unit(i).start()
    for i in (Y2, Z2):
        unit_in(i).wait_recv()
    for i in STAGES[2]:
        pass_unit(i).start()
    for c in swap_in:
        c.wait_recv()
    prepare(theirs)
    share(0, 4, 0, other).wait_recv()
    share(4, 4, 8, other).wait_recv()

    def work(k, first=False, last=False):
        made = {}

        def lanes(a, b):
            return lat[pl.ds(k * 8, 8), :, :, a:b].reshape(CHUNK, b - a)

        def scores(h):
            pair, side = h // 2, h % 2
            if pair not in made:
                cols = slice(pair * 256, (pair + 1) * 256)
                here = lanes(0, LATENT)
                keys = jnp.dot(here, wk[:, cols], preferred_element_type=F32).astype(BF16)
                vals = lax.dot_general(wvt[cols, :], here, NT, preferred_element_type=F32).astype(BF16)
                made[pair] = (keys, vals)
            keys = made[pair][0][:, side * 128 : (side + 1) * 128]
            left = jnp.concatenate([keys, lanes(LATENT, WIDE)], 1)
            right = jnp.concatenate([qn[:, h * 128 : (h + 1) * 128], qrot[h]], 1)
            s = lax.dot_general(left, right, NT, preferred_element_type=F32)
            if first or last:
                start, n = (0, OWN_FIRST * 64) if first else (OWN_FIRST * 64, OWN_LAST * 64)
                s = jnp.concatenate([s[:n] + hide[start : start + n, :], s[n:]], 0)
            return s

        def finish(h, s):
            w = jnp.exp2(s * SCALE2)
            sums = jnp.sum(w.reshape(CHUNK // 8, 8, CHUNK), 0)
            vals = made[h // 2][1][(h % 2) * 128 : (h % 2 + 1) * 128]
            gains = jnp.dot(vals, w.astype(BF16), preferred_element_type=F32)
            if not first:
                sums = total[h] + sums
                gains = acc[h] + gains
            if not last:
                total[h] = sums
                acc[h] = gains
                return None
            row = jnp.sum(sums, 0, keepdims=True)
            done[:, h * 128 : (h + 1) * 128] = (gains / row).T.astype(BF16)
            return row

        held = [scores(h) for h in range(AHEAD)]
        rows_total = []
        for h in range(HEADS):
            if h + AHEAD < HEADS:
                held.append(scores(h + AHEAD))
            rows_total.append(finish(h, held.pop(0)))
        return rows_total

    def keep(k):
        return pltpu.make_async_copy(lat.at[pl.ds(k * 8, 8)], all_hbm.at[pl.ds(k * 8, 8)], all_sem.at[k])

    keep(0).start()
    work(0, first=True)

    def step_body(k, carry):
        @pl.when(k == 1)
        def _():
            for i in range(8):
                unit_in(8 + i).wait_recv()
            share_chunk(1).start()

        for i in range(8):
            if i < 2:
                @pl.when(k < 6)
                def _():
                    unit_in(k * 8 + 8 + i).wait_recv()
            else:
                unit_in(k * 8 + 8 + i).wait_recv()
        share_chunk(k + 1).start()

        @pl.when(k == 1)
        def _():
            for i in STAGES[3]:
                pass_unit(i).start()

        @pl.when(k == 2)
        def _():
            for i in STAGES[4]:
                pass_unit(i).start()

        chunk_in(k).wait_recv()
        keep(k).start()
        work(k)
        return carry

    lax.fori_loop(1, 7, step_body, 0)

    chunk_in(7).wait_recv()
    keep(7).start()
    rows_total = work(7, last=True)

    give = pltpu.make_async_copy(done.at[mine], out_hbm.at[:, mine_cols], o_loc)
    give_away = remote(done.at[theirs], out_hbm.at[:, mine_cols], o_send.at[0], o_recv.at[0], sibling)
    give_away.start()
    give.start()
    most = functools.reduce(jnp.maximum, rows_total)
    least = functools.reduce(jnp.minimum, rows_total)
    for i in range(2):
        here = slice(i * ROWS, (i + 1) * ROWS)
        line = lax.broadcasted_iota(jnp.int32, (8, ROWS), 0)
        peak[i] = jnp.where(line < 4, most[:, here], least[:, here])
    tell = remote(peak.at[other], peak_ref.at[core], o_send.at[1], o_recv.at[1], sibling)
    tell.start()
    peak_ref[core] = peak[core]

    for c in swap:
        c.wait_send()

    def all_sent(i, carry):
        unit_in(i).wait_send()
        return carry

    lax.fori_loop(1, 64, all_sent, 0)
    share(0, 4, 0, core).wait_send()
    share(4, 4, 8, core).wait_send()
    for k in range(1, 8):
        share_chunk(k).wait_send()
    for k in range(8):
        keep(k).wait()
    give.wait()
    give_away.wait_send()
    into = out_hbm.at[:, their_cols]
    remote(into, into, o_send.at[0], o_recv.at[0], sibling).wait_recv()
    tell.wait_send()
    into = peak_ref.at[other]
    remote(into, into, o_send.at[1], o_recv.at[1], sibling).wait_recv()


def settle(
    peak_hbm, pos_ref, fast_hbm, all_hbm, qn_hbm, qr_hbm, wk_hbm, wv_hbm, out_hbm,
    peak, lat, wk, wv, qn, qr, acc, total, top, result, stage, sem, peak_sem, in_sem, out_sem,
):
    through = []
    for i in range(4):
        rows = pl.ds(i * 64, 64)
        through.append(
            (
                pltpu.make_async_copy(fast_hbm.at[rows], stage.at[rows], in_sem.at[i]),
                pltpu.make_async_copy(stage.at[rows], out_hbm.at[rows], out_sem.at[i]),
            )
        )
    for come, _ in through:
        come.start()
    look = pltpu.make_async_copy(peak_hbm, peak, peak_sem)
    look.start()
    for come, go in through:
        come.wait()
        go.start()
    look.wait()
    line = lax.broadcasted_iota(jnp.int32, (2, 8, ROWS), 1)
    low = jnp.where(peak[...] <= 1.0, 1.0, 0.0)
    high = jnp.where(peak[...] >= LEAST, 1.0, 0.0)
    bad = jnp.min(jnp.where(line < 4, low, high)) < 0.5
    for _, go in through:
        go.wait()

    @pl.when(bad)
    def _():
        core = lax.axis_index("seq") % 2
        head = lax.axis_index("head")

        def fetch(src, dst):
            c = pltpu.make_async_copy(src, dst, sem)
            c.start()
            c.wait()

        fetch(all_hbm, lat)
        qmask = query_mask(pos_ref).astype(F32)
        qlane = lax.broadcasted_iota(jnp.int32, (ROWS, 128), 1)

        def one_pair(pair, carry):
            pair_cols = at_rows(pair * 256, 256, 256)
            fetch(wk_hbm.at[:, pair_cols], wk)
            fetch(wv_hbm.at[:, pair_cols], wv)
            fetch(qn_hbm.at[:, pair_cols], qn)
            fetch(qr_hbm.at[:, at_rows(pair * 128, 128, 128)], qr)
            for side in range(2):
                cols = slice(side * 128, (side + 1) * 128)
                both = qr[...].astype(F32)
                if side:
                    both = pltpu.roll(both, ROPE, 1)
                rot = jnp.where(qlane < ROPE, both, qmask).astype(BF16)
                right = jnp.concatenate([qn[:, cols], rot], 1)
                acc[...] = jnp.zeros_like(acc)
                total[...] = jnp.zeros_like(total)
                top[...] = jnp.full_like(top, MASKED)

                def one_block(i, c):
                    rows = lat[pl.ds(i * 4, 4)].reshape(ROWS, WIDE)
                    here = rows[:, :LATENT]
                    keys = jnp.dot(here, wk[:, cols], preferred_element_type=F32).astype(BF16)
                    vals = jnp.dot(here, wv[:, cols], preferred_element_type=F32).astype(BF16)
                    left = jnp.concatenate([keys, rows[:, LATENT:]], 1)
                    s = lax.dot_general(right, left, NT, preferred_element_type=F32)
                    q = lax.broadcasted_iota(jnp.int32, (ROWS, ROWS), 0)
                    k = lax.broadcasted_iota(jnp.int32, (ROWS, ROWS), 1)
                    slot = i * 4 + k // 64
                    h = jnp.full((ROWS, ROWS), 8, jnp.int32)
                    for own in list(range(OWN_FIRST)) + list(range(56, 56 + OWN_LAST)):
                        h = jnp.where(slot == own, head_of(own, head // 2, head % 2), h)
                    own_key = h * UNIT + k % UNIT
                    same = (h < 8) & (k // UNIT % 2 == core) & (own_key // 128 == q // 128)
                    s = jnp.where(same & (own_key > q), MASKED, s) * SCALE2
                    new = jnp.maximum(top[...], jnp.max(s, 1, keepdims=True))
                    w = jnp.where(s > MASKED * SCALE2 / 2, jnp.exp2(s - new[:, :1]), 0.0)
                    factor = jnp.exp2(top[...] - new)
                    total[...] = total[...] * factor + jnp.sum(w, 1, keepdims=True)
                    acc[...] = acc[...] * factor + jnp.dot(w.astype(BF16), vals, preferred_element_type=F32)
                    top[...] = new
                    return c

                lax.fori_loop(0, 16, one_block, 0)
                result[:, cols] = (acc[...] / total[...]).astype(BF16)
            fetch(result, out_hbm.at[:, pair_cols])
            return carry

        lax.fori_loop(0, 8, one_pair, 0)


def per_device(q_nope, q_rope, latent, k_rope, positions, w_uk, w_uv):
    hbm = pl.BlockSpec(memory_space=pltpu.HBM)
    vmem = pl.BlockSpec(memory_space=pltpu.VMEM)
    smem = pl.BlockSpec(memory_space=pltpu.SMEM)
    dma = pltpu.SemaphoreType.DMA
    fast, rows, peak = pl.pallas_call(
        gather_attend,
        out_shape=(
            jax.ShapeDtypeStruct((ROWS, 2 * COLS), BF16),
            jax.ShapeDtypeStruct((64, 2, UNIT, WIDE), BF16),
            jax.ShapeDtypeStruct((2, 8, ROWS), F32),
        ),
        in_specs=[smem, vmem, vmem] + [hbm] * 4,
        out_specs=(hbm, hbm, vmem),
        scratch_shapes=[
            pltpu.VMEM((64, 2, UNIT, WIDE), BF16),
            pltpu.VMEM((LATENT, COLS), BF16),
            pltpu.VMEM((LATENT, COLS), BF16),
            pltpu.VMEM((COLS, LATENT), BF16),
            pltpu.VMEM((CHUNK, COLS), BF16),
            pltpu.VMEM((CHUNK, COLS // 2), BF16),
            pltpu.VMEM((CHUNK, 128), BF16),
            pltpu.VMEM((HEADS, CHUNK, 128), BF16),
            pltpu.VMEM(((OWN_FIRST + OWN_LAST) * 64, CHUNK), F32),
            pltpu.VMEM((HEADS, 128, CHUNK), F32),
            pltpu.VMEM((HEADS, 8, CHUNK), F32),
            pltpu.VMEM((CHUNK, COLS), BF16),
            pltpu.VMEM((2, 8, ROWS), F32),
            dma((4,)),
            dma((3,)), dma((3,)),
            dma((64,)), dma((64,)),
            dma((9,)), dma((9,)),
            dma,
            dma((2,)), dma((2,)),
            dma((8,)),
        ],
        compiler_params=pltpu.CompilerParams(
            collective_id=0, has_side_effects=True, vmem_limit_bytes=56 * 2**20
        ),
        cost_estimate=pl.CostEstimate(flops=26 * 10**9, bytes_accessed=12 * 2**20, transcendentals=17 * 10**6),
        name="gather_attend",
    )(positions, latent, k_rope, q_nope, q_rope, w_uk, w_uv)
    return pl.pallas_call(
        settle,
        out_shape=jax.ShapeDtypeStruct((ROWS, 2 * COLS), BF16),
        in_specs=[hbm, smem] + [hbm] * 6,
        out_specs=hbm,
        scratch_shapes=[
            pltpu.VMEM((2, 8, ROWS), F32),
            pltpu.VMEM((64, 2, UNIT, WIDE), BF16),
            pltpu.VMEM((LATENT, 256), BF16),
            pltpu.VMEM((LATENT, 256), BF16),
            pltpu.VMEM((ROWS, 256), BF16),
            pltpu.VMEM((ROWS, 128), BF16),
            pltpu.VMEM((ROWS, 128), F32),
            pltpu.VMEM((ROWS, 128), F32),
            pltpu.VMEM((ROWS, 128), F32),
            pltpu.VMEM((ROWS, 256), BF16),
            pltpu.VMEM((ROWS, 2 * COLS), BF16),
            dma,
            dma,
            dma((4,)),
            dma((4,)),
        ],
        compiler_params=pltpu.CompilerParams(vmem_limit_bytes=64 * 2**20 - 2**16),
        name="settle",
    )(peak, positions, fast, rows, q_nope, q_rope, w_uk, w_uv)


def solution(mesh):
    in_specs = (
        P("seq", "head"),
        P("seq", "head"),
        P(("seq", "head"), None),
        P(("seq", "head"), None),
        P("seq"),
        P(None, "head"),
        P(None, "head"),
    )
    return jax.shard_map(
        per_device, mesh=mesh, in_specs=in_specs, out_specs=P("seq", "head"), check_vma=False
    )
```

time: 83.3 us -> 272 us (3.27)
  Pallas kernels: 83.1 us -> 271 us
    pallas_call x1, Pallas kernels: 33.6 us -> 227 us  [per_device(): pl.pallas_call(settle, out_shape=jax.ShapeDtypeStruct((ROWS, 2 * COLS), B...]
    pallas_call x1, Pallas kernels: 49.5 us -> 44.3 us  [per_device(): pl.pallas_call(gather_attend, out_shape=(jax.ShapeDtypeStruct((ROWS, 2 *...]
where the time goes in v3:
time: 272 us; the launch traced here: 271 us
  Pallas kernels  271 us (100%)
    pallas_call x1, Pallas kernels, per_device(): pl.pallas_call(settle, out_shape=jax.ShapeDtypeStruct((ROWS, 2 * COLS), B...  227 us
    pallas_call x1, Pallas kernels, per_device(): pl.pallas_call(gather_attend, out_shape=(jax.ShapeDtypeStruct((ROWS, 2 *...  44.3 us

profile of v3, /device:TPU:1, one launch (start us, length us, event | category | flops | bytes accessed | tf_op | source)
XLA Modules:
  0.0 270.9 jit_solution(6275242034055851034)
XLA Ops:
  0.0 44.3 %gather_attend.1 = (bf16[256,2048]{1,0:T(8,128)(2,1)}, bf16[64,2,32,640]{3,2,1,0:T(8,128)(2,1)}, f32[2,8,256]{2,1,0:T(8,128)}) custom-call(s32[256]{0:T(256)} %pos_ref.3, bf16[32,512]{1,0:T(8,128)(2,1)} %lat_ref.1, bf16[32,64]{1,0:T(8,128)(2,1)} %rot_ref.1, bf16[256,2048]{1,0:T(8,128)(2,1)} %qn_hbm.3, bf16[256,1024]{1,0:T(8,128)(2,1)} %qr_hbm.3, ...), custom_call_target="tpu_custom_call" | custom-call | flops 25999998976 | bytes 12582912 | tf_op jit(solution)/shard_map/gather_attend/pallas_call | solution.py:473
  44.3 226.6 %settle.1 = bf16[256,2048]{1,0:T(8,128)(2,1)} custom-call(f32[2,8,256]{2,1,0:T(8,128)} %get-tuple-element.8.peak_hbm, s32[256]{0:T(256)} %pos_ref.3, bf16[256,2048]{1,0:T(8,128)(2,1)} %get-tuple-element.9.fast_hbm, bf16[64,2,32,640]{3,2,1,0:T(8,128)(2,1)} %get-tuple-element.10.all_hbm, bf16[256,2048]{1,0:T(8,128)(2,1)} %qn_hbm.3, bf16[256,1024]{1,0:T(8,128)(2,1)} %qr_hbm.3, ...), custom_call_target="tpu_custom_call" | custom-call | tf_op jit(solution)/shard_map/settle/pallas_call | solution.py:510

commit v4 on v3

--- a/solution.py
+++ b/solution.py
@@ -48,10 +48,9 @@
 Y2, Z2 = 56, 57
 OWN_FIRST, OWN_LAST = 3, 5
 STAGES = (
-    list(range(1, 8)) + [Y2, Z2],
-    list(range(8, 24)),
-    list(range(24, 32)) + [58, 59, 60],
-    list(range(32, 44)),
+    list(range(1, 8)),
+    list(range(8, 24)) + [Y2, Z2],
+    list(range(24, 44)) + [58, 59, 60],
     list(range(44, 56)) + [61, 62, 63],
 )
 
@@ -59,13 +58,9 @@
 def plan_routes():
     place = {s: i for i, s in enumerate(SLOTS)}
     routes = {i: (SLOTS[i], 0) for i in STAGES[0]}
-    first = {0} | set(STAGES[0])
-    ready = (first, first, first, first | set(STAGES[1]), first | set(STAGES[1]) | set(range(24, 32)))
-    for stages, have in (
-        (STAGES[1] + STAGES[2], first),
-        (STAGES[3], first | set(STAGES[1])),
-        (STAGES[4], first | set(STAGES[1]) | set(range(24, 32))),
-    ):
+    have = {0}
+    for stages, more in zip(STAGES[1:], (STAGES[0], STAGES[1], list(range(24, 40)))):
+        have |= set(more)
         load = {}
         options, taken = {}, {}
         for i in stages:
@@ -117,7 +112,7 @@
 
 def gather_attend(
     pos_ref, lat_ref, rot_ref, qn_hbm, qr_hbm, wk_hbm, wv_hbm,
-    out_hbm, all_hbm, peak_ref,
+    fast, all_hbm, peak_ref,
     lat, wk, wv, wvt, qn, qr, qmask, qrot, hide, acc, total, done, peak,
     loc_sem, q_send, q_recv, u_send, u_recv, d_send, d_recv, o_loc, o_send, o_recv, all_sem,
 ):
@@ -237,21 +232,19 @@
     share(4, 4, 8, core).start()
     for i in STAGES[1]:
         pass_unit(i).start()
-    for i in (Y2, Z2):
-        unit_in(i).wait_recv()
-    for i in STAGES[2]:
-        pass_unit(i).start()
     for c in swap_in:
         c.wait_recv()
     prepare(theirs)
     share(0, 4, 0, other).wait_recv()
     share(4, 4, 8, other).wait_recv()
 
-    def work(k, first=False, last=False):
+    def work(k, side_now=None, first=False, last=False):
         made = {}
 
         def lanes(a, b):
-            return lat[pl.ds(k * 8, 8), :, :, a:b].reshape(CHUNK, b - a)
+            if side_now is None:
+                return lat[pl.ds(k * 8, 8), :, :, a:b].reshape(CHUNK, b - a)
+            return lat[pl.ds(k * 8, 16), side_now, :, a:b].reshape(CHUNK, b - a)
 
         def scores(h):
             pair, side = h // 2, h % 2
@@ -300,35 +293,47 @@
     keep(0).start()
     work(0, first=True)
 
+    def arrive(slots):
+        for i in slots:
+            unit_in(i).wait_recv()
+
     def step_body(k, carry):
         @pl.when(k == 1)
         def _():
-            for i in range(8):
-                unit_in(8 + i).wait_recv()
+            arrive(list(range(8, 24)) + [Y2, Z2])
             share_chunk(1).start()
-
-        for i in range(8):
-            if i < 2:
-                @pl.when(k < 6)
-                def _():
-                    unit_in(k * 8 + 8 + i).wait_recv()
-            else:
-                unit_in(k * 8 + 8 + i).wait_recv()
-        share_chunk(k + 1).start()
-
-        @pl.when(k == 1)
+            share_chunk(2).start()
+            for i in STAGES[2]:
+                pass_unit(i).start()
+
+        @pl.when(k == 3)
         def _():
+            arrive(range(24, 40))
+            share_chunk(3).start()
+            share_chunk(4).start()
             for i in STAGES[3]:
                 pass_unit(i).start()
 
-        @pl.when(k == 2)
+        @pl.when(k == 5)
         def _():
-            for i in STAGES[4]:
-                pass_unit(i).start()
-
-        chunk_in(k).wait_recv()
-        keep(k).start()
-        work(k)
+            arrive(range(40, 56))
+            share_chunk(5).start()
+            share_chunk(6).start()
+
+        @pl.when(k == 6)
+        def _():
+            arrive(range(58, 64))
+            share_chunk(7).start()
+
+        @pl.when(k % 2 == 0)
+        def _():
+            chunk_in(k - 1).wait_recv()
+            chunk_in(k).wait_recv()
+            keep(k - 1).start()
+            keep(k).start()
+
+        late = (k + 1) % 2
+        work(k - late, side_now=core + late * (1 - 2 * core))
         return carry
 
     lax.fori_loop(1, 7, step_body, 0)
@@ -337,8 +342,8 @@
     keep(7).start()
     rows_total = work(7, last=True)
 
-    give = pltpu.make_async_copy(done.at[mine], out_hbm.at[:, mine_cols], o_loc)
-    give_away = remote(done.at[theirs], out_hbm.at[:, mine_cols], o_send.at[0], o_recv.at[0], sibling)
+    give = pltpu.make_async_copy(done.at[mine], fast.at[:, mine_cols], o_loc)
+    give_away = remote(done.at[theirs], fast.at[:, mine_cols], o_send.at[0], o_recv.at[0], sibling)
     give_away.start()
     give.start()
     most = functools.reduce(jnp.maximum, rows_total)
@@ -367,7 +372,7 @@
         keep(k).wait()
     give.wait()
     give_away.wait_send()
-    into = out_hbm.at[:, their_cols]
+    into = fast.at[:, their_cols]
     remote(into, into, o_send.at[0], o_recv.at[0], sibling).wait_recv()
     tell.wait_send()
     into = peak_ref.at[other]
@@ -375,32 +380,16 @@
 
 
 def settle(
-    peak_hbm, pos_ref, fast_hbm, all_hbm, qn_hbm, qr_hbm, wk_hbm, wv_hbm, out_hbm,
-    peak, lat, wk, wv, qn, qr, acc, total, top, result, stage, sem, peak_sem, in_sem, out_sem,
+    peak, pos_ref, fast, all_hbm, qn_hbm, qr_hbm, wk_hbm, wv_hbm, out_hbm,
+    lat, wk, wv, qn, qr, acc, total, top, result, sem, out_sem,
 ):
-    through = []
-    for i in range(4):
-        rows = pl.ds(i * 64, 64)
-        through.append(
-            (
-                pltpu.make_async_copy(fast_hbm.at[rows], stage.at[rows], in_sem.at[i]),
-                pltpu.make_async_copy(stage.at[rows], out_hbm.at[rows], out_sem.at[i]),
-            )
-        )
-    for come, _ in through:
-        come.start()
-    look = pltpu.make_async_copy(peak_hbm, peak, peak_sem)
-    look.start()
-    for come, go in through:
-        come.wait()
-        go.start()
-    look.wait()
+    whole = pltpu.make_async_copy(fast, out_hbm, out_sem)
+    whole.start()
     line = lax.broadcasted_iota(jnp.int32, (2, 8, ROWS), 1)
     low = jnp.where(peak[...] <= 1.0, 1.0, 0.0)
     high = jnp.where(peak[...] >= LEAST, 1.0, 0.0)
     bad = jnp.min(jnp.where(line < 4, low, high)) < 0.5
-    for _, go in through:
-        go.wait()
+    whole.wait()
 
     @pl.when(bad)
     def _():
@@ -473,12 +462,12 @@
     fast, rows, peak = pl.pallas_call(
         gather_attend,
         out_shape=(
-            jax.ShapeDtypeStruct((ROWS, 2 * COLS), BF16),
+            pltpu.VMEM((ROWS, 2 * COLS), BF16),
             jax.ShapeDtypeStruct((64, 2, UNIT, WIDE), BF16),
-            jax.ShapeDtypeStruct((2, 8, ROWS), F32),
+            pltpu.VMEM((2, 8, ROWS), F32),
         ),
         in_specs=[smem, vmem, vmem] + [hbm] * 4,
-        out_specs=(hbm, hbm, vmem),
+        out_specs=(vmem, hbm, vmem),
         scratch_shapes=[
             pltpu.VMEM((64, 2, UNIT, WIDE), BF16),
             pltpu.VMEM((LATENT, COLS), BF16),
@@ -502,18 +491,19 @@
             dma((8,)),
         ],
         compiler_params=pltpu.CompilerParams(
-            collective_id=0, has_side_effects=True, vmem_limit_bytes=56 * 2**20
+            collective_id=0, has_side_effects=True, vmem_limit_bytes=58 * 2**20
         ),
         cost_estimate=pl.CostEstimate(flops=26 * 10**9, bytes_accessed=12 * 2**20, transcendentals=17 * 10**6),
         name="gather_attend",
     )(positions, latent, k_rope, q_nope, q_rope, w_uk, w_uv)
+    fast = pltpu.with_memory_space_constraint(fast, pltpu.VMEM)
+    peak = pltpu.with_memory_space_constraint(peak, pltpu.VMEM)
     return pl.pallas_call(
         settle,
         out_shape=jax.ShapeDtypeStruct((ROWS, 2 * COLS), BF16),
-        in_specs=[hbm, smem] + [hbm] * 6,
+        in_specs=[vmem, smem, vmem] + [hbm] * 5,
         out_specs=hbm,
         scratch_shapes=[
-            pltpu.VMEM((2, 8, ROWS), F32),
             pltpu.VMEM((64, 2, UNIT, WIDE), BF16),
             pltpu.VMEM((LATENT, 256), BF16),
             pltpu.VMEM((LATENT, 256), BF16),
@@ -523,13 +513,10 @@
             pltpu.VMEM((ROWS, 128), F32),
             pltpu.VMEM((ROWS, 128), F32),
             pltpu.VMEM((ROWS, 256), BF16),
-            pltpu.VMEM((ROWS, 2 * COLS), BF16),
             dma,
             dma,
-            dma((4,)),
-            dma((4,)),
         ],
-        compiler_params=pltpu.CompilerParams(vmem_limit_bytes=64 * 2**20 - 2**16),
+        compiler_params=pltpu.CompilerParams(vmem_limit_bytes=59 * 2**20),
         name="settle",
     )(peak, positions, fast, rows, q_nope, q_rope, w_uk, w_uv)
 

time: 272 us -> 270 us (level)
  Pallas kernels: 271 us -> 268 us
where the time goes in v4:
time: 270 us; the launch traced here: 268 us
  Pallas kernels  268 us (99%)
    pallas_call x1, Pallas kernels, per_device(): pl.pallas_call(settle, out_shape=jax.ShapeDtypeStruct((ROWS, 2 * COLS), B...  226 us
    pallas_call x1, Pallas kernels, per_device(): pl.pallas_call(gather_attend, out_shape=(pltpu.VMEM((ROWS, 2 * COLS), BF1...  42.7 us

profile of v4, /device:TPU:1, one launch (start us, length us, event | category | flops | bytes accessed | tf_op | source)
XLA Modules:
  0.0 268.3 jit_solution(11535254624325148605)
XLA Ops:
  0.0 42.7 %gather_attend.1 = (bf16[256,2048]{1,0:T(8,128)(2,1)S(1)}, bf16[64,2,32,640]{3,2,1,0:T(8,128)(2,1)}, f32[2,8,256]{2,1,0:T(8,128)S(1)}) custom-call(s32[256]{0:T(256)} %pos_ref.3, bf16[32,512]{1,0:T(8,128)(2,1)} %lat_ref.1, bf16[32,64]{1,0:T(8,128)(2,1)} %rot_ref.1, bf16[256,2048]{1,0:T(8,128)(2,1)} %qn_hbm.3, bf16[256,1024]{1,0:T(8,128)(2,1)} %qr_hbm.3, ...), custom_call_target="tpu_custom_call" | custom-call | flops 25999998976 | bytes 12582912 | tf_op jit(solution)/shard_map/gather_attend/pallas_call | solution.py:462
  42.7 225.5 %settle.1 = bf16[256,2048]{1,0:T(8,128)(2,1)} custom-call(f32[2,8,256]{2,1,0:T(8,128)S(1)} %get-tuple-element.8.peak, s32[256]{0:T(256)} %pos_ref.3, bf16[256,2048]{1,0:T(8,128)(2,1)S(1)} %get-tuple-element.9.fast, bf16[64,2,32,640]{3,2,1,0:T(8,128)(2,1)} %get-tuple-element.10.all_hbm, bf16[256,2048]{1,0:T(8,128)(2,1)} %qn_hbm.3, bf16[256,1024]{1,0:T(8,128)(2,1)} %qr_hbm.3, ...), custom_call_target="tpu_custom_call" | custom-call | tf_op jit(solution)/shard_map/settle/pallas_call | solution.py:501

commit v5 on v4

--- a/solution.py
+++ b/solution.py
@@ -37,8 +37,8 @@
 
 SLOTS = (
     [(0, 0, 0), (0, 1, 0), (0, 3, 0), (1, 0, 0), (3, 0, 0), (0, 0, 1), (0, 0, 3), (2, 0, 0)]
-    + both_signs((1, 1, 0)) + both_signs((1, 0, 1))
-    + both_signs((0, 1, 1)) + both_signs((2, 1, 0)) + both_signs((2, 0, 1))
+    + both_signs((1, 1, 0)) + [(1, 0, 1), (3, 0, 3), (0, 1, 3), (0, 3, 1)]
+    + [(1, 0, 3), (3, 0, 1), (0, 1, 1), (0, 3, 3)] + both_signs((2, 1, 0)) + both_signs((2, 0, 1))
     + both_signs((1, 2, 0)) + both_signs((0, 2, 1)) + both_signs((1, 0, 2)) + [(2, 2, 0), (2, 0, 2)]
     + both_signs((1, 1, 1))
     + both_signs((2, 1, 1)) + both_signs((1, 2, 1))
@@ -128,14 +128,14 @@
         return (px * 4 + (pz % 2) * 2 + core, py * 2 + pz // 2)
 
     sibling = (seq + 1 - 2 * core, head)
-    partners = [chip(SLOTS[i]) for i in STAGES[0]] + [sibling]
+    near = STAGES[0] + [Y2, Z2]
+    partners = [chip(SLOTS[i]) for i in near] + [sibling]
 
     barrier = pltpu.get_barrier_semaphore()
     for p in partners:
         pl.semaphore_signal(barrier, inc=1, device_id=p, device_id_type=MESH)
 
-    mine = at_rows(core * ROWS, ROWS, ROWS)
-    theirs = at_rows(other * ROWS, ROWS, ROWS)
+    theirs, mine = pl.ds(0, ROWS), pl.ds(ROWS, ROWS)
     mine_cols = at_rows(core * COLS, COLS, COLS)
     their_cols = at_rows(other * COLS, COLS, COLS)
     half_cols = COLS // 2
@@ -185,12 +185,12 @@
     for i in STAGES[0]:
         pass_unit(i).start()
     swap = [
-        remote(qn_hbm.at[:, their_cols], qn.at[mine], q_send.at[0], q_recv.at[0], sibling),
+        remote(qn_hbm.at[:, their_cols], qn.at[theirs], q_send.at[0], q_recv.at[0], sibling),
         remote(
-            qr_hbm.at[:, at_rows(other * half_cols, half_cols, half_cols)], qr.at[mine],
+            qr_hbm.at[:, at_rows(other * half_cols, half_cols, half_cols)], qr.at[theirs],
             q_send.at[1], q_recv.at[1], sibling,
         ),
-        remote(qmask.at[mine], qmask.at[mine], q_send.at[2], q_recv.at[2], sibling),
+        remote(qmask.at[mine], qmask.at[theirs], q_send.at[2], q_recv.at[2], sibling),
     ]
     for c in swap:
         c.start()
@@ -214,6 +214,7 @@
     prepare(mine)
     key = lax.broadcasted_iota(jnp.int32, (UNIT, CHUNK), 0)
     query = lax.broadcasted_iota(jnp.int32, (UNIT, CHUNK), 1)
+    query = query + jnp.where(query < ROWS, other * ROWS, (core - 1) * ROWS)
     for n, slot in enumerate(list(range(OWN_FIRST)) + list(range(56, 56 + OWN_LAST))):
         h = head_of(slot, y, zh)
         for side in range(2):
@@ -223,6 +224,9 @@
     for i in range(HEADS):
         wvt[i * 128 : (i + 1) * 128, :] = wv[:, i * 128 : (i + 1) * 128].T
     local[1].wait()
+    for c in swap_in:
+        c.wait_recv()
+    prepare(theirs)
 
     for i in range(1, 4):
         unit_in(i).wait_recv()
@@ -232,9 +236,6 @@
     share(4, 4, 8, core).start()
     for i in STAGES[1]:
         pass_unit(i).start()
-    for c in swap_in:
-        c.wait_recv()
-    prepare(theirs)
     share(0, 4, 0, other).wait_recv()
     share(4, 4, 8, other).wait_recv()
 
@@ -246,7 +247,7 @@
                 return lat[pl.ds(k * 8, 8), :, :, a:b].reshape(CHUNK, b - a)
             return lat[pl.ds(k * 8, 16), side_now, :, a:b].reshape(CHUNK, b - a)
 
-        def scores(h):
+        def scores(h, at):
             pair, side = h // 2, h % 2
             if pair not in made:
                 cols = slice(pair * 256, (pair + 1) * 256)
@@ -256,36 +257,58 @@
                 made[pair] = (keys, vals)
             keys = made[pair][0][:, side * 128 : (side + 1) * 128]
             left = jnp.concatenate([keys, lanes(LATENT, WIDE)], 1)
-            right = jnp.concatenate([qn[:, h * 128 : (h + 1) * 128], qrot[h]], 1)
+            right = jnp.concatenate([qn[at, h * 128 : (h + 1) * 128], qrot[h, at]], 1)
             s = lax.dot_general(left, right, NT, preferred_element_type=F32)
             if first or last:
                 start, n = (0, OWN_FIRST * 64) if first else (OWN_FIRST * 64, OWN_LAST * 64)
-                s = jnp.concatenate([s[:n] + hide[start : start + n, :], s[n:]], 0)
+                s = jnp.concatenate([s[:n] + hide[start : start + n, at], s[n:]], 0)
             return s
 
-        def finish(h, s):
+        def finish(h, at, s):
             w = jnp.exp2(s * SCALE2)
-            sums = jnp.sum(w.reshape(CHUNK // 8, 8, CHUNK), 0)
+            sums = jnp.sum(w.reshape(CHUNK // 8, 8, at.stop - at.start), 0)
             vals = made[h // 2][1][(h % 2) * 128 : (h % 2 + 1) * 128]
             gains = jnp.dot(vals, w.astype(BF16), preferred_element_type=F32)
             if not first:
-                sums = total[h] + sums
-                gains = acc[h] + gains
+                sums = total[h, :, at] + sums
+                gains = acc[h, :, at] + gains
             if not last:
-                total[h] = sums
-                acc[h] = gains
+                total[h, :, at] = sums
+                acc[h, :, at] = gains
                 return None
             row = jnp.sum(sums, 0, keepdims=True)
-            done[:, h * 128 : (h + 1) * 128] = (gains / row).T.astype(BF16)
+            done[at, h * 128 : (h + 1) * 128] = (gains / row).T.astype(BF16)
             return row
 
-        held = [scores(h) for h in range(AHEAD)]
-        rows_total = []
-        for h in range(HEADS):
-            if h + AHEAD < HEADS:
-                held.append(scores(h + AHEAD))
-            rows_total.append(finish(h, held.pop(0)))
-        return rows_total
+        def sweep(at, ahead):
+            held = [scores(h, at) for h in range(ahead)]
+            rows_total = []
+            for h in range(HEADS):
+                if h + ahead < HEADS:
+                    held.append(scores(h + ahead, at))
+                rows_total.append(finish(h, at, held.pop(0)))
+            return rows_total
+
+        if not last:
+            sweep(slice(0, CHUNK), AHEAD)
+            return
+        for half in range(2):
+            rows_total = sweep(slice(half * ROWS, (half + 1) * ROWS), 2 * AHEAD - 1)
+            most = functools.reduce(jnp.maximum, rows_total)
+            least = functools.reduce(jnp.minimum, rows_total)
+            line = lax.broadcasted_iota(jnp.int32, (8, ROWS), 0)
+            both = jnp.where(line < 4, most, least)
+            if half:
+                peak_ref[0] = both
+                give.start()
+            else:
+                peak[...] = both
+                give_away.start()
+                tell.start()
+
+    give = pltpu.make_async_copy(done.at[mine], fast.at[:, mine_cols], o_loc)
+    give_away = remote(done.at[theirs], fast.at[:, mine_cols], o_send.at[0], o_recv.at[0], sibling)
+    tell = remote(peak, peak_ref.at[1], o_send.at[1], o_recv.at[1], sibling)
 
     def keep(k):
         return pltpu.make_async_copy(lat.at[pl.ds(k * 8, 8)], all_hbm.at[pl.ds(k * 8, 8)], all_sem.at[k])
@@ -340,21 +363,7 @@
 
     chunk_in(7).wait_recv()
     keep(7).start()
-    rows_total = work(7, last=True)
-
-    give = pltpu.make_async_copy(done.at[mine], fast.at[:, mine_cols], o_loc)
-    give_away = remote(done.at[theirs], fast.at[:, mine_cols], o_send.at[0], o_recv.at[0], sibling)
-    give_away.start()
-    give.start()
-    most = functools.reduce(jnp.maximum, rows_total)
-    least = functools.reduce(jnp.minimum, rows_total)
-    for i in range(2):
-        here = slice(i * ROWS, (i + 1) * ROWS)
-        line = lax.broadcasted_iota(jnp.int32, (8, ROWS), 0)
-        peak[i] = jnp.where(line < 4, most[:, here], least[:, here])
-    tell = remote(peak.at[other], peak_ref.at[core], o_send.at[1], o_recv.at[1], sibling)
-    tell.start()
-    peak_ref[core] = peak[core]
+    work(7, last=True)
 
     for c in swap:
         c.wait_send()
@@ -374,9 +383,7 @@
     give_away.wait_send()
     into = fast.at[:, their_cols]
     remote(into, into, o_send.at[0], o_recv.at[0], sibling).wait_recv()
-    tell.wait_send()
-    into = peak_ref.at[other]
-    remote(into, into, o_send.at[1], o_recv.at[1], sibling).wait_recv()
+    tell.wait()
 
 
 def settle(
@@ -481,7 +488,7 @@
             pltpu.VMEM((HEADS, 128, CHUNK), F32),
             pltpu.VMEM((HEADS, 8, CHUNK), F32),
             pltpu.VMEM((CHUNK, COLS), BF16),
-            pltpu.VMEM((2, 8, ROWS), F32),
+            pltpu.VMEM((8, ROWS), F32),
             dma((4,)),
             dma((3,)), dma((3,)),
             dma((64,)), dma((64,)),

time: 270 us -> 268 us (level)
  no operation moved by 1% of the time
where the time goes in v5:
time: 268 us; the launch traced here: 267 us
  Pallas kernels  267 us (100%)
    pallas_call x1, Pallas kernels, per_device(): pl.pallas_call(settle, out_shape=jax.ShapeDtypeStruct((ROWS, 2 * COLS), B...  225 us
    pallas_call x1, Pallas kernels, per_device(): pl.pallas_call(gather_attend, out_shape=(pltpu.VMEM((ROWS, 2 * COLS), BF1...  41.9 us

profile of v5, /device:TPU:1, one launch (start us, length us, event | category | flops | bytes accessed | tf_op | source)
XLA Modules:
  0.0 267.0 jit_solution(16612841773561009480)
XLA Ops:
  0.0 41.9 %gather_attend.1 = (bf16[256,2048]{1,0:T(8,128)(2,1)S(1)}, bf16[64,2,32,640]{3,2,1,0:T(8,128)(2,1)}, f32[2,8,256]{2,1,0:T(8,128)S(1)}) custom-call(s32[256]{0:T(256)} %pos_ref.3, bf16[32,512]{1,0:T(8,128)(2,1)} %lat_ref.1, bf16[32,64]{1,0:T(8,128)(2,1)} %rot_ref.1, bf16[256,2048]{1,0:T(8,128)(2,1)} %qn_hbm.3, bf16[256,1024]{1,0:T(8,128)(2,1)} %qr_hbm.3, ...), custom_call_target="tpu_custom_call" | custom-call | flops 25999998976 | bytes 12582912 | tf_op jit(solution)/shard_map/gather_attend/pallas_call | solution.py:469
  41.9 225.0 %settle.1 = bf16[256,2048]{1,0:T(8,128)(2,1)} custom-call(f32[2,8,256]{2,1,0:T(8,128)S(1)} %get-tuple-element.8.peak, s32[256]{0:T(256)} %pos_ref.3, bf16[256,2048]{1,0:T(8,128)(2,1)S(1)} %get-tuple-element.9.fast, bf16[64,2,32,640]{3,2,1,0:T(8,128)(2,1)} %get-tuple-element.10.all_hbm, bf16[256,2048]{1,0:T(8,128)(2,1)} %qn_hbm.3, bf16[256,1024]{1,0:T(8,128)(2,1)} %qr_hbm.3, ...), custom_call_target="tpu_custom_call" | custom-call | tf_op jit(solution)/shard_map/settle/pallas_call | solution.py:508

commit v6 on v5

--- a/solution.py
+++ b/solution.py
@@ -48,8 +48,8 @@
 Y2, Z2 = 56, 57
 OWN_FIRST, OWN_LAST = 3, 5
 STAGES = (
-    list(range(1, 8)),
-    list(range(8, 24)) + [Y2, Z2],
+    list(range(1, 8)) + [Y2, Z2],
+    list(range(8, 24)),
     list(range(24, 44)) + [58, 59, 60],
     list(range(44, 56)) + [61, 62, 63],
 )
@@ -59,7 +59,7 @@
     place = {s: i for i, s in enumerate(SLOTS)}
     routes = {i: (SLOTS[i], 0) for i in STAGES[0]}
     have = {0}
-    for stages, more in zip(STAGES[1:], (STAGES[0], STAGES[1], list(range(24, 40)))):
+    for stages, more in zip(STAGES[1:], (STAGES[0][:7], STAGES[1] + [Y2, Z2], list(range(24, 40)))):
         have |= set(more)
         load = {}
         options, taken = {}, {}
@@ -86,6 +86,7 @@
 
 
 ROUTES = plan_routes()
+FIRST_SHARES = ((0, 4, 0), (4, 3, 8), (7, 1, 9))
 
 
 def at_rows(start, size, step):
@@ -128,7 +129,7 @@
         return (px * 4 + (pz % 2) * 2 + core, py * 2 + pz // 2)
 
     sibling = (seq + 1 - 2 * core, head)
-    near = STAGES[0] + [Y2, Z2]
+    near = STAGES[0]
     partners = [chip(SLOTS[i]) for i in near] + [sibling]
 
     barrier = pltpu.get_barrier_semaphore()
@@ -228,16 +229,16 @@
         c.wait_recv()
     prepare(theirs)
 
-    for i in range(1, 4):
+    for i in STAGES[0][:7]:
         unit_in(i).wait_recv()
-    share(0, 4, 0, core).start()
-    for i in range(4, 8):
-        unit_in(i).wait_recv()
-    share(4, 4, 8, core).start()
-    for i in STAGES[1]:
-        pass_unit(i).start()
-    share(0, 4, 0, other).wait_recv()
-    share(4, 4, 8, other).wait_recv()
+        for j in STAGES[1]:
+            if ROUTES[j][1] == i:
+                pass_unit(j).start()
+        for part in FIRST_SHARES:
+            if part[0] + part[1] == i + 1:
+                share(*part, core).start()
+    for part in FIRST_SHARES:
+        share(*part, other).wait_recv()
 
     def work(k, side_now=None, first=False, last=False):
         made = {}
@@ -373,8 +374,8 @@
         return carry
 
     lax.fori_loop(1, 64, all_sent, 0)
-    share(0, 4, 0, core).wait_send()
-    share(4, 4, 8, core).wait_send()
+    for part in FIRST_SHARES:
+        share(*part, core).wait_send()
     for k in range(1, 8):
         share_chunk(k).wait_send()
     for k in range(8):
@@ -492,7 +493,7 @@
             dma((4,)),
             dma((3,)), dma((3,)),
             dma((64,)), dma((64,)),
-            dma((9,)), dma((9,)),
+            dma((10,)), dma((10,)),
             dma,
             dma((2,)), dma((2,)),
             dma((8,)),

time: 268 us -> 268 us (level)
  no operation moved by 1% of the time
where the time goes in v6:
time: 268 us; the launch traced here: 266 us
  Pallas kernels  266 us (99%)
    pallas_call x1, Pallas kernels, per_device(): pl.pallas_call(settle, out_shape=jax.ShapeDtypeStruct((ROWS, 2 * COLS), B...  225 us
    pallas_call x1, Pallas kernels, per_device(): pl.pallas_call(gather_attend, out_shape=(pltpu.VMEM((ROWS, 2 * COLS), BF1...  41.5 us

profile of v6, /device:TPU:1, one launch (start us, length us, event | category | flops | bytes accessed | tf_op | source)
XLA Modules:
  0.0 266.5 jit_solution(12427496514843229872)
XLA Ops:
  0.0 41.5 %gather_attend.1 = (bf16[256,2048]{1,0:T(8,128)(2,1)S(1)}, bf16[64,2,32,640]{3,2,1,0:T(8,128)(2,1)}, f32[2,8,256]{2,1,0:T(8,128)S(1)}) custom-call(s32[256]{0:T(256)} %pos_ref.3, bf16[32,512]{1,0:T(8,128)(2,1)} %lat_ref.1, bf16[32,64]{1,0:T(8,128)(2,1)} %rot_ref.1, bf16[256,2048]{1,0:T(8,128)(2,1)} %qn_hbm.3, bf16[256,1024]{1,0:T(8,128)(2,1)} %qr_hbm.3, ...), custom_call_target="tpu_custom_call" | custom-call | flops 25999998976 | bytes 12582912 | tf_op jit(solution)/shard_map/gather_attend/pallas_call | solution.py:470
  41.5 224.9 %settle.1 = bf16[256,2048]{1,0:T(8,128)(2,1)} custom-call(f32[2,8,256]{2,1,0:T(8,128)S(1)} %get-tuple-element.8.peak, s32[256]{0:T(256)} %pos_ref.3, bf16[256,2048]{1,0:T(8,128)(2,1)S(1)} %get-tuple-element.9.fast, bf16[64,2,32,640]{3,2,1,0:T(8,128)(2,1)} %get-tuple-element.10.all_hbm, bf16[256,2048]{1,0:T(8,128)(2,1)} %qn_hbm.3, bf16[256,1024]{1,0:T(8,128)(2,1)} %qr_hbm.3, ...), custom_call_target="tpu_custom_call" | custom-call | tf_op jit(solution)/shard_map/settle/pallas_call | solution.py:509

commit v7 on v6

--- a/solution.py
+++ b/solution.py
@@ -18,6 +18,7 @@
 WIDE = 640
 ROWS = 256
 CHUNK = 512
+PIECES = 8
 UNIT = 32
 HEADS = 8
 AHEAD = 3
@@ -301,13 +302,18 @@
             both = jnp.where(line < 4, most, least)
             if half:
                 peak_ref[0] = both
-                give.start()
+                for c in give:
+                    c.start()
             else:
                 peak[...] = both
                 give_away.start()
                 tell.start()
 
-    give = pltpu.make_async_copy(done.at[mine], fast.at[:, mine_cols], o_loc)
+    give = []
+    for i in range(PIECES):
+        size = ROWS // PIECES
+        src = done.at[pl.ds(ROWS + i * size, size)]
+        give.append(pltpu.make_async_copy(src, fast.at[pl.ds(i * size, size), mine_cols], o_loc.at[i]))
     give_away = remote(done.at[theirs], fast.at[:, mine_cols], o_send.at[0], o_recv.at[0], sibling)
     tell = remote(peak, peak_ref.at[1], o_send.at[1], o_recv.at[1], sibling)
 
@@ -380,7 +386,8 @@
         share_chunk(k).wait_send()
     for k in range(8):
         keep(k).wait()
-    give.wait()
+    for c in give:
+        c.wait()
     give_away.wait_send()
     into = fast.at[:, their_cols]
     remote(into, into, o_send.at[0], o_recv.at[0], sibling).wait_recv()
@@ -391,13 +398,18 @@
     peak, pos_ref, fast, all_hbm, qn_hbm, qr_hbm, wk_hbm, wv_hbm, out_hbm,
     lat, wk, wv, qn, qr, acc, total, top, result, sem, out_sem,
 ):
-    whole = pltpu.make_async_copy(fast, out_hbm, out_sem)
-    whole.start()
+    pieces = []
+    for i in range(PIECES):
+        rows = pl.ds(i * (ROWS // PIECES), ROWS // PIECES)
+        pieces.append(pltpu.make_async_copy(fast.at[rows], out_hbm.at[rows], out_sem.at[i]))
+    for c in pieces:
+        c.start()
     line = lax.broadcasted_iota(jnp.int32, (2, 8, ROWS), 1)
     low = jnp.where(peak[...] <= 1.0, 1.0, 0.0)
     high = jnp.where(peak[...] >= LEAST, 1.0, 0.0)
     bad = jnp.min(jnp.where(line < 4, low, high)) < 0.5
-    whole.wait()
+    for c in pieces:
+        c.wait()
 
     @pl.when(bad)
     def _():
@@ -494,7 +506,7 @@
             dma((3,)), dma((3,)),
             dma((64,)), dma((64,)),
             dma((10,)), dma((10,)),
-            dma,
+            dma((PIECES,)),
             dma((2,)), dma((2,)),
             dma((8,)),
         ],
@@ -522,7 +534,7 @@
             pltpu.VMEM((ROWS, 128), F32),
             pltpu.VMEM((ROWS, 256), BF16),
             dma,
-            dma,
+            dma((PIECES,)),
         ],
         compiler_params=pltpu.CompilerParams(vmem_limit_bytes=59 * 2**20),
         name="settle",

time: 268 us -> 268 us (level)
  no operation moved by 1% of the time
where the time goes in v7:
time: 268 us; the launch traced here: 267 us
  Pallas kernels  267 us (100%)
    pallas_call x1, Pallas kernels, per_device(): pl.pallas_call(settle, out_shape=jax.ShapeDtypeStruct((ROWS, 2 * COLS), B...  226 us
    pallas_call x1, Pallas kernels, per_device(): pl.pallas_call(gather_attend, out_shape=(pltpu.VMEM((ROWS, 2 * COLS), BF1...  41.6 us

profile of v7, /device:TPU:1, one launch (start us, length us, event | category | flops | bytes accessed | tf_op | source)
XLA Modules:
  0.0 267.2 jit_solution(7167183595094105463)
XLA Ops:
  0.0 41.6 %gather_attend.1 = (bf16[256,2048]{1,0:T(8,128)(2,1)S(1)}, bf16[64,2,32,640]{3,2,1,0:T(8,128)(2,1)}, f32[2,8,256]{2,1,0:T(8,128)S(1)}) custom-call(s32[256]{0:T(256)} %pos_ref.3, bf16[32,512]{1,0:T(8,128)(2,1)} %lat_ref.1, bf16[32,64]{1,0:T(8,128)(2,1)} %rot_ref.1, bf16[256,2048]{1,0:T(8,128)(2,1)} %qn_hbm.3, bf16[256,1024]{1,0:T(8,128)(2,1)} %qr_hbm.3, ...), custom_call_target="tpu_custom_call" | custom-call | flops 25999998976 | bytes 12582912 | tf_op jit(solution)/shard_map/gather_attend/pallas_call | solution.py:482
  41.6 225.6 %settle.1 = bf16[256,2048]{1,0:T(8,128)(2,1)} custom-call(f32[2,8,256]{2,1,0:T(8,128)S(1)} %get-tuple-element.8.peak, s32[256]{0:T(256)} %pos_ref.3, bf16[256,2048]{1,0:T(8,128)(2,1)S(1)} %get-tuple-element.9.fast, bf16[64,2,32,640]{3,2,1,0:T(8,128)(2,1)} %get-tuple-element.10.all_hbm, bf16[256,2048]{1,0:T(8,128)(2,1)} %qn_hbm.3, bf16[256,1024]{1,0:T(8,128)(2,1)} %qr_hbm.3, ...), custom_call_target="tpu_custom_call" | custom-call | tf_op jit(solution)/shard_map/settle/pallas_call | solution.py:521
